TPU v7x, 256 devices: a whole 4x4x8 slice. The times are simulated.
256 devices in a mesh: ctx: 128 (over x, y, z_lo, core), mp: 2 (over z_hi).
Axes of the slice: x: 4, y: 4, z: 8 (z_hi: 2, z_lo: 4; z = z_hi * 4 + z_lo), core: 2. Of those that a mesh axis runs over, the one named last changes fastest.
Arguments:
- query_rows: bfloat16 [32768, 768], P('ctx', 'mp'), may hold values from -6 to 6
- key_rows: bfloat16 [32768, 768], P('ctx', 'mp'), may hold values from -6 to 6
- value_rows: bfloat16 [32768, 768], P('ctx', 'mp'), may hold values from -6 to 6
- w_output: bfloat16 [768, 768], P('mp'), may hold values from -0.21875 to 0.21875
- grad_output: bfloat16 [32768, 768], P('ctx', 'mp'), may hold values from -6 to 6
Outputs:
- layer_out: bfloat16 [32768, 768], P('ctx', 'mp')
- grad_query: bfloat16 [32768, 768], P('ctx', 'mp')
- grad_key: bfloat16 [32768, 768], P('ctx', 'mp')
- grad_value: bfloat16 [32768, 768], P('ctx', 'mp')
- grad_weight: float32 [768, 768], P('mp')
All inputs are finite; a program needn't handle non-finite values.
Results may differ from a plain program's by a relative error of at most 0.0091.
Values may be sent and summed in bfloat16 or wider, within the bound.
A program may use at most 128 MiB of HBM per device.

v0:
```python
import jax
import jax.numpy as jnp
from jax import lax
from jax.sharding import PartitionSpec as P

HEAD = 64
BLOCK = 64


def swapped(block, axis, stride):
    count = lax.axis_size(axis)
    route = []
    for low in range(count):
        high = low | 1 << stride
        if high != low and high < count:
            route += [(low, high), (high, low)]
    return lax.ppermute(block, axis, route)


def pool_rows(stacked):
    halves = stacked.astype(jnp.float32).reshape(
        (stacked.shape[0], stacked.shape[1] // 2, 2) + stacked.shape[2:]
    )
    return ((halves[:, :, 0] + halves[:, :, 1]) * 0.5).astype(jnp.bfloat16)


def spread_rows(gradient):
    return 0.5 * jnp.repeat(gradient, 2, axis=1)


def flip_groups(grouped):
    shape = grouped.shape
    paired = grouped.reshape((shape[0], shape[1] // 2, 2) + shape[2:])
    return paired[:, :, ::-1].reshape(shape)


def join_pair(mine, other, upper_flag):
    lower = jnp.where(upper_flag == 0, mine, other)
    upper = jnp.where(upper_flag == 0, other, mine)
    return jnp.concatenate([lower, upper], axis=1)


def attend(queries, key_sets, grad_attn):
    count, heads_here, head_size = queries.shape
    scale = HEAD ** (-0.5)
    grouped_list = []
    score_list = []
    for stacked in key_sets:
        groups = stacked.shape[1]
        grouped = queries.reshape(groups, count // groups, heads_here, head_size)
        grouped_list.append(grouped)
        scores = jnp.einsum(
            "gqhe,gkhe->gqhk", grouped, stacked[0], preferred_element_type=jnp.float32
        )
        score_list.append(scores.reshape(count, heads_here, stacked.shape[2]))
    scores = jnp.concatenate(score_list, axis=-1) * scale
    largest = jnp.max(scores, axis=-1, keepdims=True)
    weights = jnp.exp(scores - largest)
    probs = weights / jnp.sum(weights, axis=-1, keepdims=True)
    probs_low = probs.astype(jnp.bfloat16)
    grad_low = grad_attn.astype(jnp.bfloat16)
    width = key_sets[0].shape[2]
    outputs = jnp.zeros(queries.shape, jnp.float32)
    pieces = []
    grad_list = []
    for index, stacked in enumerate(key_sets):
        groups = stacked.shape[1]
        piece = probs_low[:, :, index * width : (index + 1) * width].reshape(
            groups, count // groups, heads_here, width
        )
        grad_grouped = grad_low.reshape(groups, count // groups, heads_here, head_size)
        pieces.append((piece, grad_grouped))
        outputs = outputs + jnp.einsum(
            "gqhk,gkhe->gqhe", piece, stacked[1], preferred_element_type=jnp.float32
        ).reshape(queries.shape)
        grad_list.append(
            jnp.einsum(
                "gqhe,gkhe->gqhk", grad_grouped, stacked[1], preferred_element_type=jnp.float32
            ).reshape(count, heads_here, width)
        )
    grad_probs = jnp.concatenate(grad_list, axis=-1)
    centre = jnp.sum(probs * grad_probs, axis=-1, keepdims=True)
    grad_scores = (probs * (grad_probs - centre) * scale).astype(jnp.bfloat16)
    grad_queries = jnp.zeros(queries.shape, jnp.float32)
    grad_sets = []
    for index, stacked in enumerate(key_sets):
        groups = stacked.shape[1]
        piece, grad_grouped = pieces[index]
        grad_piece = grad_scores[:, :, index * width : (index + 1) * width].reshape(
            groups, count // groups, heads_here, width
        )
        grad_queries = grad_queries + jnp.einsum(
            "gqhk,gkhe->gqhe", grad_piece, stacked[0], preferred_element_type=jnp.float32
        ).reshape(queries.shape)
        grad_keys = jnp.einsum(
            "gqhk,gqhe->gkhe", grad_piece, grouped_list[index], preferred_element_type=jnp.float32
        )
        grad_values = jnp.einsum(
            "gqhk,gqhe->gkhe", piece, grad_grouped, preferred_element_type=jnp.float32
        )
        grad_sets.append(jnp.stack([grad_keys, grad_values]))
    return (outputs, grad_queries, grad_sets)


def on_device(query_rows, key_rows, value_rows, w_output, grad_output):
    row_count, columns = query_rows.shape
    heads_here = columns // HEAD
    local = (row_count // BLOCK).bit_length() - 1
    bits = lax.axis_size("ctx").bit_length() - 1
    place = lax.axis_index("ctx")
    full_grad = lax.all_gather(grad_output, "mp", axis=1, tiled=True)
    grad_attn = lax.dot_general(
        full_grad, w_output, (((1,), (1,)), ((), ())), preferred_element_type=jnp.float32
    )
    stacked = jnp.stack([key_rows, value_rows]).reshape(2, row_count, heads_here, HEAD)
    pyramid = [stacked]
    for level in range(local):
        pyramid.append(pool_rows(pyramid[-1]))
    base = pyramid[local]
    siblings = []
    mine = base
    for bit in range(bits):
        other = swapped(mine, "ctx", bit)
        siblings.append(other)
        if bit + 1 < bits:
            mine = pool_rows(join_pair(mine, other, place >> bit & 1))
    queries = query_rows.reshape(row_count, heads_here, HEAD)
    grad_attn3 = grad_attn.reshape(row_count, heads_here, HEAD)
    own_set = stacked.reshape(2, row_count // BLOCK, BLOCK, heads_here, HEAD)
    local_sets = [
        flip_groups(pyramid[level].reshape(2, -1, BLOCK, heads_here, HEAD))
        for level in range(local)
    ]
    far_sets = [sibling[:, None] for sibling in siblings]
    local_parts = [[] for level in range(local)]
    far_grads = [jnp.zeros((2, 1, BLOCK, heads_here, HEAD), jnp.float32) for sibling in siblings]
    sets = [own_set]
    for level in range(local):
        sets.append(local_sets[level])
    sets = sets + far_sets
    outputs, grad_queries, grad_sets = attend(queries, sets, grad_attn3)
    own_parts = grad_sets[0]
    for level in range(local):
        local_parts[level].append(grad_sets[1 + level])
    for index in range(len(siblings)):
        far_grads[index] = grad_sets[1 + local + index]
    attn = outputs.reshape(row_count, columns).astype(jnp.bfloat16)
    partial_value = jnp.dot(attn, w_output, preferred_element_type=jnp.float32)
    layer_out = lax.psum_scatter(partial_value, "mp", scatter_dimension=1, tiled=True).astype(
        jnp.bfloat16
    )
    weight_terms = lax.dot_general(
        attn, full_grad, (((0,), (0,)), ((), ())), preferred_element_type=jnp.float32
    )
    grad_weight = lax.psum(weight_terms, "ctx")
    sibling_grads = [grad[:, 0] for grad in far_grads]
    chain_grad = jnp.zeros(base.shape, jnp.float32)
    for bit in reversed(range(bits)):
        upper_flag = place >> bit & 1
        outgoing = sibling_grads[bit]
        own_share = jnp.zeros(base.shape, jnp.float32)
        if bit + 1 < bits:
            halves = spread_rows(chain_grad)
            lower_half = halves[:, :BLOCK]
            upper_half = halves[:, BLOCK:]
            own_share = jnp.where(upper_flag == 0, lower_half, upper_half)
            outgoing = outgoing + jnp.where(upper_flag == 0, upper_half, lower_half)
        chain_grad = swapped(outgoing, "ctx", bit) + own_share
    carried = chain_grad
    for level in reversed(range(local)):
        level_grad = flip_groups(jnp.concatenate(local_parts[level], axis=1)).reshape(
            2, -1, heads_here, HEAD
        )
        carried = level_grad + spread_rows(carried)
    carried = carried + own_parts.reshape(2, row_count, heads_here, HEAD)
    grad_query = grad_queries.reshape(row_count, columns).astype(jnp.bfloat16)
    grad_key = carried[0].reshape(row_count, columns).astype(jnp.bfloat16)
    grad_value = carried[1].reshape(row_count, columns).astype(jnp.bfloat16)
    return (layer_out, grad_query, grad_key, grad_value, grad_weight)


def solution(mesh):
    placed = (P("ctx", "mp"), P("ctx", "mp"), P("ctx", "mp"), P("mp", None), P("ctx", "mp"))
    return jax.shard_map(
        on_device,
        mesh=mesh,
        in_specs=placed,
        out_specs=(P("ctx", "mp"), P("ctx", "mp"), P("ctx", "mp"), P("ctx", "mp"), P("mp", None)),
        check_vma=False,
    )
```

profile of v0, /device:TPU:1, one launch (start us, length us, event | category | flops | bytes accessed | tf_op | source)
XLA Modules:
  0.0 1432.5 jit_solution(371576495384934286)
XLA Ops:
  12.8 3.2 collective-permute-start
  17.4 11.3 all_gather.3
  36.9 4.9 slice.291
  45.2 1.4 slice.294
  48.2 1.4 copy.434
  51.7 1.8 constant_dynamic-update-slice_fusion.1
  53.5 4.9 slice.262
  61.9 1.4 slice.267
  63.4 1.9 constant_dynamic-update-slice_fusion.2
  66.2 1.8 constant_dynamic-update-slice_fusion
  71.2 4.0 collective-permute-start.1
  75.2 1.9 fusion.17
  79.6 4.0 collective-permute-start.2
  84.0 9.2 collective-permute-done.2
  95.7 4.4 collective-permute-done.3
  101.1 2.9 collective-permute-start.4
  104.3 3.3 collective-permute-done.4
  110.2 3.1 collective-permute-done.5
  114.2 2.7 collective-permute-start.6
  117.3 3.0 collective-permute-done.6
  120.5 2.3 fusion.135
  132.6 3.0 collective-permute-start.7
  135.6 1.9 reshape.616
  137.5 2.0 copy.466
  139.5 1.9 reshape.643
  141.4 1.9 reshape.615
  143.3 2.0 copy.463
  145.3 2.3 fusion.50
  147.6 1.4 fusion.136
  149.0 2.2 fusion.10
  151.2 2.3 copy.468
  153.5 2.3 add.184
  164.2 2.1 pad_maximum_fusion.1
  166.3 2.1 reverse.7
  168.4 2.1 copy.518
  170.5 2.4 reshape_reshape.11
  172.8 1.9 reshape.644
  174.7 2.1 copy.499
  176.8 2.6 fusion.9
  179.3 2.3 copy.496
  181.7 2.4 add.195
  184.1 1.9 convolution_bitcast_fusion.29
  186.0 2.3 fusion.54
  188.2 2.1 fusion.59
  203.6 5.9 collective-permute-done.8
  209.9 3.0 collective-permute-start.9
  213.3 5.4 collective-permute-done.9
  219.2 1.4 collective-permute-start.10
  221.6 7.7 collective-permute-done.10
  232.2 2.1 copy.511
  234.4 1.8 copy.512
  236.2 3.1 pad_maximum_fusion
  239.3 2.2 collective-permute-done.11
  244.7 4.6 collective-permute-start.12
  249.2 1.8 convolution_bitcast_fusion.39
  251.0 9.5 rev.2
  260.5 3.3 reshape_reshape.10
  263.8 2.3 copy.531
  266.1 2.3 stack.135
  271.2 5.4 collective-permute-start.13
  282.5 1.4 fusion.27
  285.5 1.7 convert_element_type.192
  287.2 1135.3 %all-reduce.2.cloned.1.call-done = f32[384,768]{1,0:T(8,128)} async-done(((f32[384,768]{1,0:T(8,128)}), f32[384,768]{1,0:T(8,128)}) %all-reduce.2.cloned.1.call-update) | async-done | bytes 1179664 | tf_op jit(solution)/shard_map/psum | solution.py:155
  1422.6 2.4 copy.649
  (259 shorter events, 89.1 us)
Async XLA Ops:
  8.0 20.7 %copy-start = (bf16[384,768]{1,0:T(8,128)(2,1)S(1)}, bf16[384,768]{1,0:T(8,128)(2,1)}, u32[]{:S(2)}) copy-start(bf16[384,768]{1,0:T(8,128)(2,1)} %param.8) | copy-start | bytes 1769476
  8.0 277.5 %reduce-scatter.2.cloned.1.call-start = ((), (), s32[]{:S(2)}) async-start(), calls=%async_computation.1 | async-start | bytes 1179648 | tf_op jit(solution)/shard_map/reduce_scatter | solution.py:149
  11.0 5.1 copy-start.34
  11.0 6.4 copy-start.43
  11.2 19.4 %copy-start.35 = (bf16[256,384]{1,0:T(8,128)(2,1)S(1)}, bf16[256,384]{1,0:T(8,128)(2,1)}, u32[]{:S(2)}) copy-start(bf16[256,384]{1,0:T(8,128)(2,1)} %param.6) | copy-start | bytes 589828
  12.1 20.7 %copy-start.42 = (bf16[256,384]{1,0:T(8,128)(2,1)S(1)}, bf16[256,384]{1,0:T(8,128)(2,1)}, u32[]{:S(2)}) copy-start(bf16[256,384]{1,0:T(8,128)(2,1)} %param.5) | copy-start | bytes 589828
  12.8 56.3 %collective-permute-start = (bf16[2,64,6,64]{3,1,2,0:T(8,128)(2,1)}, bf16[2,64,6,64]{3,1,2,0:T(8,128)(2,1)}, u32[]{:S(2)}, u32[]{:S(2)}) collective-permute-start(bf16[2,64,6,64]{3,1,2,0:T(8,128)(2,1)} %fusion.61), channel_id=1, source_target_pairs={{0,2},{2,0},{4,6},{6,4},{8,10},{10,8},{12,14},{14,12},{16,18},{18,... | collective-permute-start | bytes 294920 | tf_op jit(solution)/shard_map/ppermute | solution.py:17
  28.7 0.8 copy-start.9
  34.9 6.9 copy-start.13
  42.1 4.6 copy-start.12
  46.8 18.4 %copy-start.18 = (bf16[2,64,6,64]{3,1,2,0:T(8,128)(2,1)}, bf16[2,64,6,64]{3,1,2,0:T(8,128)(2,1)S(1)}, u32[]{:S(2)}) copy-start(bf16[2,64,6,64]{3,1,2,0:T(8,128)(2,1)S(1)} %copy.488) | copy-start | bytes 294916
  48.2 10.8 copy-start.1
  49.6 8.8 copy-start.14
  58.7 9.4 copy-start.11
  58.7 9.4 copy-start.16
  63.4 7.8 copy-start.20
  69.1 7.9 copy-start.8
  71.2 7.5 collective-permute-start.1
  77.0 6.6 copy-start.44
  78.7 15.4 %copy-start.22 = (bf16[2,64,6,64]{3,1,2,0:T(8,128)(2,1)}, bf16[2,64,6,64]{3,1,2,0:T(8,128)(2,1)S(1)}, u32[]{:S(2)}) copy-start(bf16[2,64,6,64]{3,1,2,0:T(8,128)(2,1)S(1)} %collective-permute-done.1) | copy-start | bytes 294916
  79.6 13.5 collective-permute-start.2
  93.1 7.9 copy-start.24
  94.1 6.0 collective-permute-start.3
  100.1 8.4 copy-start.25
  101.1 6.6 collective-permute-start.4
  107.7 6.5 copy-start.26
  108.6 4.6 collective-permute-start.5
  113.2 7.1 copy-start.27
  114.2 6.1 collective-permute-start.6
  120.3 2.8 copy-start.39
  123.3 4.5 copy-start.17
  124.7 1.3 copy-start.6
  124.7 4.1 copy-start.21
  124.7 6.1 copy-start.19
  132.6 68.8 %collective-permute-start.7 = (f32[2,64,6,64]{3,1,2,0:T(8,128)}, f32[2,64,6,64]{3,1,2,0:T(8,128)}, u32[]{:S(2)}, u32[]{:S(2)}) collective-permute-start(f32[2,64,6,64]{3,1,2,0:T(8,128)} %maximum_bitcast_fusion.6), channel_id=1, source_target_pairs={{0,128},{128,0},{2,130},{130,2},{4,132},{132,4},{6,134},{134,6},{8... | collective-permute-start | bytes 589832 | tf_op jit(solution)/shard_map/ppermute | solution.py:17
  147.6 10.8 copy-start.23
  155.8 6.2 copy-start.28
  155.8 6.5 copy-start.40
  155.8 6.8 copy-start.31
  164.2 1258.4 %all-reduce.2.cloned.1.call-start = ((), (), s32[]{:S(2)}) async-start(), calls=%async_computation.2 | async-start | bytes 2359296 | tf_op jit(solution)/shard_map/psum | solution.py:155
  184.1 6.3 copy-start.2
  184.1 6.3 copy-start.15
  184.1 7.5 copy-start.10
  192.8 7.6 copy-start.41
  192.9 7.6 copy-start.7
  192.9 7.8 copy-start.29
  192.9 7.8 copy-start.30
  200.5 2.3 copy-start.36
  202.8 6.7 collective-permute-start.8
  209.9 8.8 collective-permute-start.9
  219.2 10.2 collective-permute-start.10
  229.7 0.9 copy-start.4
  231.4 10.2 collective-permute-start.11
  234.4 7.2 copy-start.5
  234.4 9.4 copy-start.37
  234.4 9.4 copy-start.38
  242.9 0.9 copy-start.3
  244.7 23.9 %collective-permute-start.12 = (f32[2,64,6,64]{3,1,2,0:T(8,128)}, f32[2,64,6,64]{3,1,2,0:T(8,128)}, u32[]{:S(2)}, u32[]{:S(2)}) collective-permute-start(f32[2,64,6,64]{3,1,2,0:T(8,128)} %fusion.45), channel_id=1, source_target_pairs={{0,4},{4,0},{2,6},{6,2},{8,12},{12,8},{10,14},{14,10},{16,20},{20,... | collective-permute-start | bytes 589832 | tf_op jit(solution)/shard_map/ppermute | solution.py:17
  271.2 9.2 collective-permute-start.13
  277.9 3.2 copy-start.32
  280.8 1.6 copy-start.33
Sparse Core Ops, SparseCore 0:
  164.3 38.8 reduce-scatter.1
Sparse Core Ops, SparseCore 1:
  193.0 1229.5 all-reduce.1
where the time goes:
time: 1440 us; the launch traced here: 1430 us
  waiting for transfers between devices  1180 us (82%)
  local copies, waits for them, and re-layouts  114 us (8%)
  matrix products  49.8 us (3%)
  starting transfers between devices  37.1 us (3%)
  other arithmetic  23.6 us (2%)
  between operations  16.9 us (1%)
    psum x1, waiting for transfers between devices, on_device(): grad_weight = lax.psum(weight_terms, 'ctx')  1140 us
    ppermute x14, waiting for transfers between devices, swapped(): return lax.ppermute(block, axis, route)  44.6 us
    ppermute x14, starting transfers between devices, swapped(): return lax.ppermute(block, axis, route)  37 us
  transfers between devices with their start and end apart: 16, of which 11 were waited for; matrix products, arithmetic and copies ran while one was open for 11% of the time, Pallas kernels for 0%

commit v1 on v0

v1 whole, which is shorter than its diff:
```python
import functools

import jax
import jax.numpy as jnp
from jax import lax
from jax.experimental import pallas as pl
from jax.experimental.pallas import tpu as pltpu
from jax.sharding import PartitionSpec as P

HEAD = 64
BLOCK = 64
NEAR = 8
NEAR_BITS = 3
MESH = pl.DeviceIdType.MESH
BF = jnp.bfloat16
F32 = jnp.float32


def iota(shape, axis):
    return lax.broadcasted_iota(jnp.int32, shape, axis)


def where_one(condition, weight):
    return jnp.where(condition, weight, 0.0).astype(BF)


def mm(a, b):
    return jnp.dot(a, b, preferred_element_type=F32)


def mm_nt(a, b):
    return lax.dot_general(a, b, (((1,), (1,)), ((), ())), preferred_element_type=F32)


def pool(rows):
    count = rows.shape[0]
    out = max(count // 2, 16)
    halves = where_one(iota((out, count), 1) // 2 == iota((out, count), 0), 0.5)
    return mm(halves, rows).astype(BF)


def sibling(index):
    return index + 1 - 2 * (index % 2)


def kernel(
    hi_bits,
    q_ref, k_ref, v_ref, w_ref, go_ref,
    lo_out, dq_out, dk_out, dv_out, gw_out,
    near_rows, level1, far, far_f32, ug, up, up_f32, fg, bdq, bdo, probs, attn_t, dq_t,
    d_far, d_send, d_f32, r1_land, r1_f32, msg, r2_land, d_loc, d_l1,
    gw_send, gw_land, gw_part, gw_ar, gw_all, lo_send, lo_land,
    f1_s, f1_r, f1u_s, f1u_r, f2_s, f2_r, r1_s, r1_r, r1g_s, r1g_r,
    r2_s, r2_r, r2g_s, r2g_r, ag_s, ag_r, mp_s, mp_r,
):
    his = 1 << hi_bits
    sets = NEAR_BITS + hi_bits
    keys = sets * BLOCK
    wide = 2 * 384
    place = lax.axis_index("ctx")
    mp = lax.axis_index("mp")
    hi = place // NEAR
    lo = place % NEAR

    def near_id(e):
        return (hi * NEAR + e, mp)

    def far_id(f):
        return (f * NEAR + lo, mp)

    mp_id = (place, 1 - mp)

    def near_copy(b, j, src, dst, send, recv):
        n = 1 << b
        e = sibling(lo // n) * n + j
        return pltpu.make_async_remote_copy(
            src_ref=src, dst_ref=dst, send_sem=send.at[n - 1 + j], recv_sem=recv.at[n - 1 + lo % n],
            device_id=near_id(e), device_id_type=MESH)

    def far_copy(b, j, src, dst, send, recv):
        n = 1 << b
        f = sibling(hi // n) * n + j
        return pltpu.make_async_remote_copy(
            src_ref=src, dst_ref=dst, send_sem=send.at[n - 1 + j], recv_sem=recv.at[n - 1 + hi % n],
            device_id=far_id(f), device_id_type=MESH)

    def each(n, mine, body):
        if n == 1:
            body(0)
        else:
            def step(t, c):
                body((t + mine) % n)
                return c
            lax.fori_loop(0, n, step, 0)

    def wait_in(dst, recv):
        pltpu.make_async_copy(dst, dst, recv).wait()

    barrier = pltpu.get_barrier_semaphore()
    for b in range(NEAR_BITS):
        n = 1 << b
        each(n, lo, lambda j, n=n: pl.semaphore_signal(
            barrier, inc=1, device_id=near_id(sibling(lo // n) * n + j), device_id_type=MESH))
    for b in range(hi_bits):
        n = 1 << b
        each(n, hi, lambda j, n=n: pl.semaphore_signal(
            barrier, inc=1, device_id=far_id(sibling(hi // n) * n + j), device_id_type=MESH))
    pl.semaphore_signal(barrier, inc=1, device_id=mp_id, device_id_type=MESH)

    rows = jnp.concatenate([k_ref[...], v_ref[...]], axis=1)
    rows = pool(rows)
    level1[...] = rows
    rows = pool(rows)
    near_rows[0:64, :] = rows
    rows = pool(rows)
    near_rows[64:96, :] = rows
    rows = pool(rows)
    near_rows[96:112, :] = rows
    first = pool(rows)
    step_up = where_one(iota((16, 16), 1) // 2 + 8 == iota((16, 16), 0), 0.5)
    upper = first
    for _ in range(3):
        upper = (first.astype(F32) + mm(step_up, upper)).astype(BF)
    near_rows[112:128, :] = upper
    ug[lo] = upper
    fg[mp] = go_ref[...]

    pl.semaphore_wait(barrier, NEAR - 1 + his - 1 + 1)

    near_at = (0, 64, 96)

    for b in range(NEAR_BITS):
        n, r = 1 << b, BLOCK >> b
        each(n, lo, lambda j, b=b: near_copy(
            b, j, near_rows.at[pl.ds(112, 16)], ug.at[lo], f1u_s, f1u_r).start())
    for b in range(NEAR_BITS):
        n, r = 1 << b, BLOCK >> b
        each(n, lo, lambda j, b=b, n=n, r=r: near_copy(
            b, j, near_rows.at[pl.ds(near_at[b], r)],
            far.at[pl.ds(pl.multiple_of(b * BLOCK + (lo % n) * r, 16), r)], f1_s, f1_r).start())

    lane_low = iota((128, 128), 1) < HEAD
    masks = (where_one(lane_low, 1.0), where_one(jnp.logical_not(lane_low), 1.0))

    def local_rows(own, i, p, side):
        lanes = slice(i * 128, i * 128 + 128)
        upper_lanes = slice(side * 384 + i * 128, side * 384 + i * 128 + 128)
        return jnp.concatenate(
            [own[p * 128:p * 128 + 128, lanes], level1[64 * (1 - p):64 * (1 - p) + 64, upper_lanes]], axis=0)

    for i in range(3):
        for p in range(2):
            part = q_ref[p * 128:p * 128 + 128, i * 128:i * 128 + 128]
            for h in range(2):
                at = p * 256 + h * 128
                bdq[i, at:at + 128, :] = part * masks[h]
        for p in range(2):
            probs[i, keys:keys + 192, p * 256:p * 256 + 256] = mm_nt(
                local_rows(k_ref, i, p, 0), bdq[i, p * 256:p * 256 + 256, :])

    for b in range(NEAR_BITS):
        n = 1 << b
        each(n, lo, lambda j, n=n: wait_in(
            ug.at[sibling(lo // n) * n + j], f1u_r.at[n - 1 + j]))
    gathered = ug[...].reshape(NEAR * 16, wide)
    a = iota((128, 128), 0)
    source = jnp.where(
        a < 64, a // 8 * 16 + a % 8,
        jnp.where(a < 96, (a - 64) // 4 * 16 + 8 + a % 4,
                  jnp.where(a < 112, (a - 96) // 2 * 16 + 12 + a % 2, (a - 112) * 16 + 14)))
    levels = mm(where_one(iota((128, 128), 1) == source, 1.0), gathered)
    up[...] = levels[0:112].astype(BF)
    up_f32[...] = levels[112:120]

    up_at = (0, 64, 96)
    for b in reversed(range(hi_bits)):
        n, r = 1 << b, BLOCK >> b
        if b < 3:
            each(n, hi, lambda j, b=b, n=n, r=r: far_copy(
                b, j, up.at[pl.ds(up_at[b], r)],
                far.at[pl.ds(pl.multiple_of((NEAR_BITS + b) * BLOCK + (hi % n) * r, 16), r)], f2_s, f2_r).start())
        else:
            each(n, hi, lambda j, b=b, n=n, r=r: far_copy(
                b, j, up_f32, far_f32.at[pl.ds(pl.multiple_of((hi % n) * r, 8), r)], f2_s, f2_r).start())
    to_mp = pltpu.make_async_remote_copy(
        src_ref=go_ref, dst_ref=fg.at[mp], send_sem=mp_s.at[0], recv_sem=mp_r.at[0],
        device_id=mp_id, device_id_type=MESH)
    to_mp.start()

    for b in range(NEAR_BITS):
        n, r = 1 << b, BLOCK >> b
        each(n, lo, lambda j, b=b, n=n, r=r: wait_in(
            far.at[pl.ds(pl.multiple_of(b * BLOCK + j * r, 16), r)], f1_r.at[n - 1 + j]))
    for i in range(3):
        probs[i, 0:192, :] = mm_nt(far[0:192, i * 128:i * 128 + 128], bdq[i])

    for b in range(hi_bits):
        n, r = 1 << b, BLOCK >> b
        if b < 3:
            each(n, hi, lambda j, b=b, n=n, r=r: wait_in(
                far.at[pl.ds(pl.multiple_of((NEAR_BITS + b) * BLOCK + j * r, 16), r)], f2_r.at[n - 1 + j]))
        else:
            each(n, hi, lambda j, b=b, n=n, r=r: wait_in(
                far_f32.at[pl.ds(pl.multiple_of(j * r, 8), r)], f2_r.at[n - 1 + j]))
            far[6 * BLOCK:7 * BLOCK, :] = far_f32[...].astype(BF)

    unit = HEAD ** -0.5 * 1.4426950408889634
    for i in range(3):
        probs[i, 192:keys, :] = mm_nt(far[192:keys, i * 128:i * 128 + 128], bdq[i])
        v_far_t = far[:, 384 + i * 128:384 + i * 128 + 128].T
        for p in range(2):
            v_loc_t = local_rows(v_ref, i, p, 1).T
            for h in range(2):
                lanes = slice(p * 256 + h * 128, p * 256 + h * 128 + 128)
                scores = probs[i, :, lanes] * unit
                largest = jnp.max(scores, axis=0, keepdims=True)
                weights = jnp.exp2(scores - largest)
                weights = weights * (1.0 / jnp.sum(weights, axis=0, keepdims=True))
                probs[i, :, lanes] = weights
                low = weights.astype(BF)
                part = mm(v_far_t[h * 64:h * 64 + 64], low[:keys]) + mm(v_loc_t[h * 64:h * 64 + 64], low[keys:])
                attn_t[i * 128 + h * 64:i * 128 + h * 64 + 64, p * 128:p * 128 + 128] = part.astype(BF)

    wait_in(fg.at[1 - mp], mp_r.at[0])
    tall = 384 // (his // 2)
    for c in range(2):
        terms = mm(attn_t[...], fg[c]).astype(BF)
        for t in range(his // 2):
            gw_send[2 * t + c] = terms[t * tall:t * tall + tall]
    gw_land[hi] = gw_send[hi]
    for b in range(hi_bits):
        n = 1 << b
        each(n, hi, lambda j, b=b, n=n: far_copy(
            b, j, gw_send.at[sibling(hi // n) * n + j], gw_land.at[hi], r1g_s, r1g_r).start())
    attn = attn_t[...].T
    lo_send[...] = mm(attn, w_ref[:, pl.ds(pl.multiple_of((1 - mp) * 384, 128), 384)]).astype(BF)
    to_lo = pltpu.make_async_remote_copy(
        src_ref=lo_send, dst_ref=lo_land, send_sem=mp_s.at[1], recv_sem=mp_r.at[1],
        device_id=mp_id, device_id_type=MESH)
    to_lo.start()

    grad_attn = (mm_nt(fg[0], w_ref[:, 0:384]) + mm_nt(fg[1], w_ref[:, 384:768])).astype(BF)
    for i in range(3):
        for p in range(2):
            part = grad_attn[p * 128:p * 128 + 128, i * 128:i * 128 + 128]
            for h in range(2):
                at = p * 256 + h * 128
                bdo[i, at:at + 128, :] = part * masks[h]
        k_lanes = slice(i * 128, i * 128 + 128)
        v_lanes = slice(384 + i * 128, 384 + i * 128 + 128)
        gp_far = mm_nt(far[:, v_lanes], bdo[i])
        k_far_t = far[:, k_lanes].T
        d_scores, p_low = [], []
        for p in range(2):
            gp_loc = mm_nt(local_rows(v_ref, i, p, 1), bdo[i, p * 256:p * 256 + 256, :])
            k_loc_t = local_rows(k_ref, i, p, 0).T
            ds_half, pl_half = [], []
            for h in range(2):
                lanes = slice(p * 256 + h * 128, p * 256 + h * 128 + 128)
                weights = probs[i, :, lanes]
                grads = jnp.concatenate([gp_far[:, lanes], gp_loc[:, h * 128:h * 128 + 128]], axis=0)
                centre = jnp.sum(weights * grads, axis=0, keepdims=True)
                ds = (weights * (grads - centre) * HEAD ** -0.5).astype(BF)
                part = mm(k_far_t[h * 64:h * 64 + 64], ds[:keys]) + mm(k_loc_t[h * 64:h * 64 + 64], ds[keys:])
                dq_t[i * 128 + h * 64:i * 128 + h * 64 + 64, p * 128:p * 128 + 128] = part
                ds_half.append(ds)
                pl_half.append(weights.astype(BF))
            ds_p = jnp.concatenate(ds_half, axis=1)
            pl_p = jnp.concatenate(pl_half, axis=1)
            dk_l = mm(ds_p[keys:], bdq[i, p * 256:p * 256 + 256, :])
            dv_l = mm(pl_p[keys:], bdo[i, p * 256:p * 256 + 256, :])
            d_loc[p * 128:p * 128 + 128, k_lanes] = dk_l[0:128]
            d_loc[p * 128:p * 128 + 128, v_lanes] = dv_l[0:128]
            d_l1[64 * (1 - p):64 * (1 - p) + 64, k_lanes] = dk_l[128:192].astype(BF)
            d_l1[64 * (1 - p):64 * (1 - p) + 64, v_lanes] = dv_l[128:192].astype(BF)
            d_scores.append(ds_p[:keys])
            p_low.append(pl_p[:keys])
        dk_f = mm(jnp.concatenate(d_scores, axis=1), bdq[i])
        dv_f = mm(jnp.concatenate(p_low, axis=1), bdo[i])
        d_far[:, k_lanes] = dk_f[0:192]
        d_far[:, v_lanes] = dv_f[0:192]
        low_keys = min(keys, 384)
        d_send[:, k_lanes] = dk_f[192:low_keys].astype(BF)
        d_send[:, v_lanes] = dv_f[192:low_keys].astype(BF)
        if hi_bits > 3:
            d_f32[:, k_lanes] = dk_f[384:448]
            d_f32[:, v_lanes] = dv_f[384:448]

    for b in range(hi_bits):
        n, r = 1 << b, BLOCK >> b
        if b < 3:
            each(n, hi, lambda j, b=b, n=n, r=r: far_copy(
                b, j, d_send.at[pl.ds(pl.multiple_of(b * BLOCK + j * r, 16), r)],
                r1_land.at[pl.ds(pl.multiple_of(b * BLOCK + (hi % n) * r, 16), r)], r1_s, r1_r).start())
        else:
            each(n, hi, lambda j, b=b, n=n, r=r: far_copy(
                b, j, d_f32.at[pl.ds(pl.multiple_of(j * r, 8), r)],
                r1_f32.at[pl.ds(pl.multiple_of((hi % n) * r, 8), r)], r1_s, r1_r).start())

    for b in range(hi_bits):
        n = 1 << b
        each(n, hi, lambda j, n=n: wait_in(gw_land.at[sibling(hi // n) * n + j], r1g_r.at[n - 1 + j]))
    total = gw_land[0].astype(F32)
    for f in range(1, his):
        total = total + gw_land[f].astype(F32)
    gw_part[...] = total.astype(BF)
    gw_ar[lo] = gw_part[...]
    for b in range(NEAR_BITS):
        n = 1 << b
        each(n, lo, lambda j, b=b: near_copy(b, j, gw_part, gw_ar.at[lo], r2g_s, r2g_r).start())

    dq_out[...] = dq_t[...].T.astype(BF)

    for b in range(hi_bits):
        n, r = 1 << b, BLOCK >> b
        if b < 3:
            each(n, hi, lambda j, b=b, n=n, r=r: wait_in(
                r1_land.at[pl.ds(pl.multiple_of(b * BLOCK + j * r, 16), r)], r1_r.at[n - 1 + j]))
        else:
            each(n, hi, lambda j, b=b, n=n, r=r: wait_in(
                r1_f32.at[pl.ds(pl.multiple_of(j * r, 8), r)], r1_r.at[n - 1 + j]))
    cols = BLOCK * hi_bits
    landed = r1_land[...]
    if hi_bits > 3:
        landed = jnp.concatenate([landed, r1_f32[...].astype(BF)], axis=0)
    at_row, at_col = iota((64, cols), 0), iota((64, cols), 1)
    spread = jnp.zeros((64, cols), F32)
    for b in range(hi_bits):
        hit = (at_col // 64 == b) & (at_row // (1 << b) == at_col % (64 >> b))
        spread = jnp.where(hit, 0.5 ** b, spread)
    group_grad = mm(spread.astype(BF), landed).astype(BF)
    at_row, at_col = iota((192, 64), 0), iota((192, 64), 1)
    spread = jnp.zeros((192, 64), F32)
    for b in range(NEAR_BITS):
        base = sibling(lo // (1 << b)) * (1 << b)
        hit = (at_row // 64 == b) & (at_col == 8 * base + at_row % 64 // (8 >> b))
        spread = jnp.where(hit, 0.5 ** (3 - b), spread)
    msg[...] = (d_far[...] + mm(spread.astype(BF), group_grad)).astype(BF)

    for b in range(NEAR_BITS):
        n, r = 1 << b, BLOCK >> b
        each(n, lo, lambda j, b=b, n=n, r=r: near_copy(
            b, j, msg.at[pl.ds(pl.multiple_of(b * BLOCK + j * r, 16), r)],
            r2_land.at[pl.ds(pl.multiple_of(b * BLOCK + (lo % n) * r, 16), r)], r2_s, r2_r).start())

    for b in range(NEAR_BITS):
        n = 1 << b
        each(n, lo, lambda j, n=n: wait_in(gw_ar.at[sibling(lo // n) * n + j], r2g_r.at[n - 1 + j]))
    total = gw_ar[0].astype(F32)
    for e in range(1, NEAR):
        total = total + gw_ar[e].astype(F32)
    gw_part2 = total.astype(BF)
    gw_all[hi] = gw_part2
    for b in range(hi_bits):
        n = 1 << b
        each(n, hi, lambda j, b=b: far_copy(b, j, gw_all.at[hi], gw_all.at[hi], ag_s, ag_r).start())

    for b in range(NEAR_BITS):
        n, r = 1 << b, BLOCK >> b
        each(n, lo, lambda j, b=b, n=n, r=r: wait_in(
            r2_land.at[pl.ds(pl.multiple_of(b * BLOCK + j * r, 16), r)], r2_r.at[n - 1 + j]))
    terms = jnp.concatenate([r2_land[...], group_grad, d_l1[...]], axis=0)
    at_row, at_col = iota((256, 384), 0), iota((256, 384), 1)
    spread = jnp.zeros((256, 384), F32)
    for b in range(NEAR_BITS):
        hit = (at_col // 64 == b) & (at_row // (4 << b) == at_col % (64 >> b))
        spread = jnp.where(hit, 0.25 * 0.5 ** b, spread)
    spread = jnp.where((at_col // 64 == 3) & (at_col % 64 == 8 * lo + at_row // 32), 0.5 ** 5, spread)
    spread = jnp.where((at_col >= 256) & (at_col - 256 == at_row // 2), 0.5, spread)
    grads = d_loc[...] + mm(spread.astype(BF), terms)
    dk_out[...] = grads[:, 0:384].astype(BF)
    dv_out[...] = grads[:, 384:768].astype(BF)

    mine = mm(attn, w_ref[:, pl.ds(pl.multiple_of(mp * 384, 128), 384)])
    wait_in(lo_land, mp_r.at[1])
    lo_out[...] = (mine + lo_land[...].astype(F32)).astype(BF)

    for b in range(hi_bits):
        n = 1 << b
        each(n, hi, lambda j, n=n: wait_in(gw_all.at[sibling(hi // n) * n + j], ag_r.at[n - 1 + j]))
    for f in range(his):
        gw_out[f // 2 * tall:f // 2 * tall + tall, f % 2 * 384:f % 2 * 384 + 384] = gw_all[f].astype(F32)

    for b in range(NEAR_BITS):
        n, r = 1 << b, BLOCK >> b

        def near_done(j, b=b, n=n, r=r):
            wait_in(near_rows.at[pl.ds(112, 16)], f1u_s.at[n - 1 + j])
            wait_in(near_rows.at[pl.ds(near_at[b], r)], f1_s.at[n - 1 + j])
            wait_in(msg.at[pl.ds(pl.multiple_of(b * BLOCK + j * r, 16), r)], r2_s.at[n - 1 + j])
            wait_in(gw_part, r2g_s.at[n - 1 + j])

        each(n, lo, near_done)
    for b in range(hi_bits):
        n, r = 1 << b, BLOCK >> b

        def far_done(j, b=b, n=n, r=r):
            if b < 3:
                wait_in(up.at[pl.ds(up_at[b], r)], f2_s.at[n - 1 + j])
                wait_in(d_send.at[pl.ds(pl.multiple_of(b * BLOCK + j * r, 16), r)], r1_s.at[n - 1 + j])
            else:
                wait_in(up_f32, f2_s.at[n - 1 + j])
                wait_in(d_f32.at[pl.ds(pl.multiple_of(j * r, 8), r)], r1_s.at[n - 1 + j])
            wait_in(gw_send.at[sibling(hi // n) * n + j], r1g_s.at[n - 1 + j])
            wait_in(gw_all.at[hi], ag_s.at[n - 1 + j])

        each(n, hi, far_done)
    to_mp.wait_send()
    to_lo.wait_send()


def on_device(query_rows, key_rows, value_rows, w_output, grad_output):
    hi_bits = (lax.axis_size("ctx") // NEAR).bit_length() - 1
    his = 1 << hi_bits
    keys = (NEAR_BITS + hi_bits) * BLOCK
    low_rows = 64 * min(hi_bits, 3)
    tall = 384 // (his // 2)
    vm = pltpu.VMEM
    dma = pltpu.SemaphoreType.DMA
    near_sem, far_sem = dma((NEAR - 1,)), dma((his - 1,))
    scratch = [
        vm((128, 768), BF),
        vm((128, 768), BF),
        vm((keys, 768), BF),
        vm((64, 768), F32),
        vm((NEAR, 16, 768), BF),
        vm((112, 768), BF),
        vm((8, 768), F32),
        vm((2, 256, 384), BF),
        vm((3, 512, 128), BF),
        vm((3, 512, 128), BF),
        vm((3, keys + 192, 512), F32),
        vm((384, 256), BF),
        vm((384, 256), F32),
        vm((192, 768), F32),
        vm((low_rows, 768), BF),
        vm((64, 768), F32),
        vm((low_rows, 768), BF),
        vm((64, 768), F32),
        vm((192, 768), BF),
        vm((192, 768), BF),
        vm((256, 768), F32),
        vm((128, 768), BF),
        vm((his, tall, 384), BF),
        vm((his, tall, 384), BF),
        vm((tall, 384), BF),
        vm((NEAR, tall, 384), BF),
        vm((his, tall, 384), BF),
        vm((256, 384), BF),
        vm((256, 384), BF),
        near_sem, near_sem, near_sem, near_sem,
        far_sem, far_sem, far_sem, far_sem, far_sem, far_sem,
        near_sem, near_sem, near_sem, near_sem,
        far_sem, far_sem,
        dma((2,)), dma((2,)),
    ]
    rows = jax.ShapeDtypeStruct((256, 384), BF)
    whole = pl.BlockSpec(memory_space=pltpu.VMEM)
    return pl.pallas_call(
        functools.partial(kernel, hi_bits),
        out_shape=(rows, rows, rows, rows, jax.ShapeDtypeStruct((384, 768), F32)),
        in_specs=[whole] * 5,
        out_specs=(whole,) * 5,
        scratch_shapes=scratch,
        compiler_params=pltpu.CompilerParams(
            collective_id=0, has_side_effects=True, vmem_limit_bytes=48 * 1024 * 1024),
        cost_estimate=pl.CostEstimate(flops=1_200_000_000, bytes_accessed=4_000_000, transcendentals=1_000_000),
    )(query_rows, key_rows, value_rows, w_output, grad_output)


def solution(mesh):
    placed = (P("ctx", "mp"), P("ctx", "mp"), P("ctx", "mp"), P("mp", None), P("ctx", "mp"))
    return jax.shard_map(
        on_device,
        mesh=mesh,
        in_specs=placed,
        out_specs=(P("ctx", "mp"), P("ctx", "mp"), P("ctx", "mp"), P("ctx", "mp"), P("mp", None)),
        check_vma=False,
    )
```

time: 1440 us -> 70.1 us (0.05)
  waiting for transfers between devices: 1180 us -> 0 us
  local copies, waits for them, and re-layouts: 114 us -> 8.48 us
  Pallas kernels: 0 us -> 59.8 us
  matrix products: 49.8 us -> 0 us
  starting transfers between devices: 37.1 us -> 0 us
  other arithmetic: 23.6 us -> 0 us
  between operations: 16.9 us -> 0.66 us
    psum x1 -> x0, waiting for transfers between devices: 1140 us -> none  [on_device(): grad_weight = lax.psum(weight_terms, 'ctx')]
    pallas_call x0 -> x1, Pallas kernels: none -> 59.8 us  [on_device(): pl.pallas_call(functools.partial(kernel, hi_bits), out_shape=(rows, rows,...]
    dot_general x63 -> x0, matrix products: 49.8 us -> none  [the longest x10 13.6 us: attend(): jnp.einsum('gqhk,gkhe->gqhe', grad_piece, stacked[0], preferred_element_t...]
    ppermute x14 -> x0, waiting for transfers between devices: 44.6 us -> none  [swapped(): return lax.ppermute(block, axis, route)]
    ppermute x14 -> x0, starting transfers between devices: 37 us -> none  [swapped(): return lax.ppermute(block, axis, route)]
    another operation x15 -> x0, local copies, waits for them, and re-layouts: 24.7 us -> none  [the longest x4 7.51 us: attend(): grad_sets.append(jnp.stack([grad_keys, grad_values]))]
    slice x15 -> x0, local copies, waits for them, and re-layouts: 21.2 us -> none  [the longest x4 8.32 us: attend(): stacked[1]]
    reshape x10 -> x0, local copies, waits for them, and re-layouts: 15.7 us -> none  [the longest x4 7.75 us: attend(): probs_low[:, :, index * width:(index + 1) * width]]
  transfers between devices with their start and end apart: 16 -> 0, of which waited for: 11 -> 0; matrix products, arithmetic and copies ran while one was open for 11% -> 0% of each run, Pallas kernels for 0% -> 0%
where the time goes in v1:
time: 70.1 us; the launch traced here: 68.9 us
  Pallas kernels  59.8 us (85%)
  local copies, waits for them, and re-layouts  8.48 us (12%)
    pallas_call x1, Pallas kernels, on_device(): pl.pallas_call(functools.partial(kernel, hi_bits), out_shape=(rows, rows,...  59.8 us
    unnamed x15, local copies, waits for them, and re-layouts  8.48 us

profile of v1, /device:TPU:1, one launch (start us, length us, event | category | flops | bytes accessed | tf_op | source)
XLA Modules:
  0.0 68.9 jit_solution(14725631695313643853)
XLA Ops:
  0.6 0.0 copy-start
  0.6 1.1 %copy-done = bf16[384,768]{1,0:T(8,128)(2,1)S(1)} copy-done((bf16[384,768]{1,0:T(8,128)(2,1)S(1)}, bf16[384,768]{1,0:T(8,128)(2,1)}, u32[]{:S(2)}) %copy-start) | copy-done | bytes 589848
  1.7 0.0 copy-start.1
  1.7 0.9 %copy-done.1 = bf16[256,384]{1,0:T(8,128)(2,1)S(1)} copy-done((bf16[256,384]{1,0:T(8,128)(2,1)S(1)}, bf16[256,384]{1,0:T(8,128)(2,1)}, u32[]{:S(2)}) %copy-start.1) | copy-done | bytes 196632
  2.6 0.0 copy-start.2
  2.6 0.9 %copy-done.2 = bf16[256,384]{1,0:T(8,128)(2,1)S(1)} copy-done((bf16[256,384]{1,0:T(8,128)(2,1)S(1)}, bf16[256,384]{1,0:T(8,128)(2,1)}, u32[]{:S(2)}) %copy-start.2) | copy-done | bytes 196632
  3.6 0.0 copy-start.3
  3.6 0.9 %copy-done.3 = bf16[256,384]{1,0:T(8,128)(2,1)S(1)} copy-done((bf16[256,384]{1,0:T(8,128)(2,1)S(1)}, bf16[256,384]{1,0:T(8,128)(2,1)}, u32[]{:S(2)}) %copy-start.3) | copy-done | bytes 196632
  4.5 0.0 copy-start.4
  4.5 0.9 %copy-done.4 = bf16[256,384]{1,0:T(8,128)(2,1)S(1)} copy-done((bf16[256,384]{1,0:T(8,128)(2,1)S(1)}, bf16[256,384]{1,0:T(8,128)(2,1)}, u32[]{:S(2)}) %copy-start.4) | copy-done | bytes 196632
  5.4 59.8 %shard_map.92 = (bf16[256,384]{1,0:T(8,128)(2,1)S(1)}, bf16[256,384]{1,0:T(8,128)(2,1)S(1)}, bf16[256,384]{1,0:T(8,128)(2,1)S(1)}, bf16[256,384]{1,0:T(8,128)(2,1)S(1)}, f32[384,768]{1,0:T(8,128)S(1)}) custom-call(bf16[256,384]{1,0:T(8,128)(2,1)S(1)} %copy-done.1, bf16[256,384]{1,0:T(8,128)(2,1)S(1)} %copy-done.2, bf16[256,384]{1,0:T(8,128)(2,1)S(1)} %copy-done.3, ...), custom_call_target="tpu_custom_call" | custom-call | flops 1200000000 | bytes 4000000 | tf_op jit(solution)/shard_map/pallas_call | solution.py:459
  65.2 0.7 copy.15
  65.9 0.7 copy.16
  66.6 0.7 copy.17
  67.3 0.7 copy.18
  67.9 1.0 %copy.19 = f32[384,768]{1,0:T(8,128)} copy(f32[384,768]{1,0:T(8,128)S(1)} %get-tuple-element.14) | data formatting | bytes 2359296
Async XLA Ops:
  0.6 1.1 %copy-start = (bf16[384,768]{1,0:T(8,128)(2,1)S(1)}, bf16[384,768]{1,0:T(8,128)(2,1)}, u32[]{:S(2)}) copy-start(bf16[384,768]{1,0:T(8,128)(2,1)} %w_ref.1) | copy-start | bytes 1769476
  1.7 0.9 %copy-start.1 = (bf16[256,384]{1,0:T(8,128)(2,1)S(1)}, bf16[256,384]{1,0:T(8,128)(2,1)}, u32[]{:S(2)}) copy-start(bf16[256,384]{1,0:T(8,128)(2,1)} %q_ref.1) | copy-start | bytes 589828
  2.6 0.9 %copy-start.2 = (bf16[256,384]{1,0:T(8,128)(2,1)S(1)}, bf16[256,384]{1,0:T(8,128)(2,1)}, u32[]{:S(2)}) copy-start(bf16[256,384]{1,0:T(8,128)(2,1)} %k_ref.1) | copy-start | bytes 589828
  3.6 0.9 %copy-start.3 = (bf16[256,384]{1,0:T(8,128)(2,1)S(1)}, bf16[256,384]{1,0:T(8,128)(2,1)}, u32[]{:S(2)}) copy-start(bf16[256,384]{1,0:T(8,128)(2,1)} %v_ref.1) | copy-start | bytes 589828
  4.5 0.9 %copy-start.4 = (bf16[256,384]{1,0:T(8,128)(2,1)S(1)}, bf16[256,384]{1,0:T(8,128)(2,1)}, u32[]{:S(2)}) copy-start(bf16[256,384]{1,0:T(8,128)(2,1)} %go_ref.1) | copy-start | bytes 589828

commit v2 on v1

v2 whole, which is shorter than its diff:
```python
import jax
import jax.numpy as jnp
from jax import lax
from jax.experimental import pallas as pl
from jax.experimental.pallas import tpu as pltpu
from jax.sharding import PartitionSpec as P

HEAD = 64
BLOCK = 64
NEAR = 8
NEAR_BITS = 3
FAR = 16
FAR_BITS = 4
KEYS = (NEAR_BITS + FAR_BITS) * BLOCK
CHUNK = 24
MESH = pl.DeviceIdType.MESH
BF = jnp.bfloat16
F32 = jnp.float32


def iota(shape, axis):
    return lax.broadcasted_iota(jnp.int32, shape, axis)


def where_one(condition, weight):
    return jnp.where(condition, weight, 0.0).astype(BF)


def mm(a, b):
    return jnp.dot(a, b, preferred_element_type=F32)


def mm_nt(a, b):
    return lax.dot_general(a, b, (((1,), (1,)), ((), ())), preferred_element_type=F32)


def pool(rows):
    count = rows.shape[0]
    out = max(count // 2, 16)
    halves = where_one(iota((out, count), 1) // 2 == iota((out, count), 0), 0.5)
    return mm(halves, rows).astype(BF)


def sibling(index):
    return index + 1 - 2 * (index % 2)


def kernel(
    q_hbm, k_hbm, v_hbm, w_hbm, go_hbm,
    lo_hbm, dq_hbm, dk_hbm, dv_hbm, gw_hbm,
    lo_out, dq_out, dk_out, dv_out,
    q_ref, k_ref, v_ref, w_ref, go_ref,
    near_rows, level1, far, far_f32, ug, up, up_f32, fg, bdq, bdo, probs, attn_t, dq_t,
    d_far, d_x, d_land, d_near, d_send, d_f32, r1_land, r1_f32, gg, msg0, msg, r2_land, d_loc, d_l1,
    gw_x, gw_pl, gw_own, gw_send, gw_land, gw_part, gw_ar, gw_all, lo_send, lo_land,
    ld, st, f1_s, f1_r, f2_s, f2_r, r1_s, r1_r, r2_s, r2_r, gw_s, gw_r, pair_s, pair_r, mp_s, mp_r,
):
    place = lax.axis_index("ctx")
    mp = lax.axis_index("mp")
    hi = place // NEAR
    lo = place % NEAR
    core = lo % 2
    depth = lo // 2

    def near_id(e):
        return (hi * NEAR + e, mp)

    def far_id(f):
        return (f * NEAR + lo, mp)

    mp_id = (place, 1 - mp)

    def send(src, dst, s, r, to):
        pltpu.make_async_remote_copy(
            src_ref=src, dst_ref=dst, send_sem=s, recv_sem=r, device_id=to, device_id_type=MESH).start()

    def near_peer(b, j):
        return sibling(lo // (1 << b)) * (1 << b) + j

    def far_peer(b, j):
        return sibling(hi // (1 << b)) * (1 << b) + j

    def each(n, mine, body):
        if n <= 2:
            for j in range(n):
                body((j + mine) % n)
        else:
            def step(t, c):
                body((t + mine) % n)
                return c
            lax.fori_loop(0, n, step, 0)

    def landed_in(ref, sem):
        pltpu.make_async_copy(ref, ref, sem).wait()

    loads = [pltpu.make_async_copy(src, dst, ld.at[n]) for n, (src, dst) in enumerate(
        ((k_hbm, k_ref), (v_hbm, v_ref), (go_hbm, go_ref), (q_hbm, q_ref), (w_hbm, w_ref)))]
    for load in loads:
        load.start()
    stores = [pltpu.make_async_copy(src, dst, st.at[n]) for n, (src, dst) in enumerate(
        ((lo_out, lo_hbm), (dq_out, dq_hbm), (dk_out, dk_hbm), (dv_out, dv_hbm), (gw_all, gw_hbm)))]
    barrier = pltpu.get_barrier_semaphore()
    for b in range(NEAR_BITS):
        each(1 << b, lo, lambda j, b=b: pl.semaphore_signal(
            barrier, inc=1, device_id=near_id(near_peer(b, j)), device_id_type=MESH))
    for b in range(FAR_BITS):
        each(1 << b, hi, lambda j, b=b: pl.semaphore_signal(
            barrier, inc=1, device_id=far_id(far_peer(b, j)), device_id_type=MESH))
    pl.semaphore_signal(barrier, inc=1, device_id=mp_id, device_id_type=MESH)

    loads[0].wait()
    loads[1].wait()
    rows = jnp.concatenate([k_ref[...], v_ref[...]], axis=1)

    def keep(ref, start, rows):
        for side in range(2):
            ref[side, start:start + rows.shape[0], :] = rows[:, side * 384:side * 384 + 384]

    rows = pool(rows)
    keep(level1, 0, rows)
    rows = pool(rows)
    keep(near_rows, 0, rows)
    rows = pool(rows)
    keep(near_rows, 64, rows)
    rows = pool(rows)
    keep(near_rows, 96, rows)
    first = pool(rows)
    step_up = where_one(iota((16, 16), 1) // 2 + 8 == iota((16, 16), 0), 0.5)
    upper = first
    for _ in range(3):
        upper = (first.astype(F32) + mm(step_up, upper)).astype(BF)
    keep(near_rows, 112, upper)
    ug[lo] = near_rows[core, 112:128, :]

    pl.semaphore_wait(barrier, NEAR - 1 + FAR - 1 + 1)

    for b in range(NEAR_BITS):
        each(1 << b, lo, lambda j, b=b: send(
            near_rows.at[near_peer(b, j) % 2, pl.ds(112, 16)], ug.at[lo], f1_s.at[0], f1_r.at[0],
            near_id(near_peer(b, j))))
    each(2, lo, lambda j: send(
        near_rows.at[j, pl.ds(64, 32)],
        far.at[j, pl.ds(pl.multiple_of(64 + core * 32, 16), 32)], f1_s.at[1], f1_r.at[1], near_id(near_peer(1, j))))
    each(4, lo, lambda j: send(
        near_rows.at[j % 2, pl.ds(96, 16)],
        far.at[j % 2, pl.ds(pl.multiple_of(128 + lo % 4 * 16, 16), 16)], f1_s.at[1], f1_r.at[1],
        near_id(near_peer(2, j))))
    partner = near_id(sibling(lo))
    send(near_rows.at[:, pl.ds(0, 64)], far.at[:, pl.ds(0, 64)], pair_s.at[0], pair_r.at[0], partner)

    lane_low = iota((128, 128), 1) < HEAD
    masks = (where_one(lane_low, 1.0), where_one(jnp.logical_not(lane_low), 1.0))

    def local_rows(own, i, p, side):
        lanes = slice(i * 128, i * 128 + 128)
        return jnp.concatenate(
            [own[p * 128:p * 128 + 128, lanes], level1[side, 64 * (1 - p):64 * (1 - p) + 64, lanes]], axis=0)

    loads[3].wait()
    loads[4].wait()
    for i in range(3):
        for p in range(2):
            part = q_ref[p * 128:p * 128 + 128, i * 128:i * 128 + 128]
            for h in range(2):
                at = p * 256 + h * 128
                bdq[i, at:at + 128, :] = part * masks[h]
        for p in range(2):
            probs[i, KEYS:KEYS + 192, p * 256:p * 256 + 256] = mm_nt(
                local_rows(k_ref, i, p, 0), bdq[i, p * 256:p * 256 + 256, :])

    landed_in(ug.at[pl.ds(0, NEAR - 1)], f1_r.at[0])
    gathered = ug[...].reshape(NEAR * 16, 384)
    a = iota((128, 128), 0)
    source = jnp.where(
        a < 64, a // 8 * 16 + a % 8,
        jnp.where(a < 96, (a - 64) // 4 * 16 + 8 + a % 4,
                  jnp.where(a < 112, (a - 96) // 2 * 16 + 12 + a % 2, (a - 112) * 16 + 14)))
    levels = mm(where_one(iota((128, 128), 1) == source, 1.0), gathered)
    up[...] = levels[0:112].astype(BF)
    up_f32[...] = levels[112:120]

    each(8, hi, lambda j: send(
        up_f32, far_f32.at[pl.ds(pl.multiple_of(hi % 8 * 8, 8), 8)], f2_s.at[1], f2_r.at[1], far_id(far_peer(3, j))))
    for b in reversed(range(3)):
        r = BLOCK >> b
        each(1 << b, hi, lambda j, b=b, r=r: send(
            up.at[pl.ds((0, 64, 96)[b], r)],
            far.at[core, pl.ds(pl.multiple_of((3 + b) * BLOCK + hi % (1 << b) * r, 16), r)],
            f2_s.at[0], f2_r.at[0], far_id(far_peer(b, j))))

    loads[2].wait()
    to_mp = pltpu.make_async_remote_copy(
        src_ref=go_ref, dst_ref=fg.at[mp], send_sem=mp_s.at[0], recv_sem=mp_r.at[0],
        device_id=mp_id, device_id_type=MESH)
    to_mp.start()
    fg[mp] = go_ref[...]

    landed_in(far.at[core, pl.ds(64, 128)], f1_r.at[1])
    send(far.at[core, pl.ds(64, 128)], far.at[core, pl.ds(64, 128)], pair_s.at[1], pair_r.at[1], partner)
    landed_in(far.at[:, pl.ds(0, 64)], pair_r.at[0])
    landed_in(far.at[1 - core, pl.ds(64, 128)], pair_r.at[1])
    for i in range(3):
        probs[i, 0:192, :] = mm_nt(far[0, 0:192, i * 128:i * 128 + 128], bdq[i])

    landed_in(far_f32, f2_r.at[1])
    far[core, 384:448, :] = far_f32[...].astype(BF)
    landed_in(far.at[core, pl.ds(192, 192)], f2_r.at[0])
    send(far.at[core, pl.ds(192, 256)], far.at[core, pl.ds(192, 256)], pair_s.at[2], pair_r.at[2], partner)
    landed_in(far.at[1 - core, pl.ds(192, 256)], pair_r.at[2])

    unit = HEAD ** -0.5 * 1.4426950408889634
    for i in range(3):
        probs[i, 192:KEYS, :] = mm_nt(far[0, 192:KEYS, i * 128:i * 128 + 128], bdq[i])
        v_far_t = far[1, :, i * 128:i * 128 + 128].T
        for p in range(2):
            v_loc_t = local_rows(v_ref, i, p, 1).T
            for h in range(2):
                lanes = slice(p * 256 + h * 128, p * 256 + h * 128 + 128)
                scores = probs[i, :, lanes] * unit
                largest = jnp.max(scores, axis=0, keepdims=True)
                weights = jnp.exp2(scores - largest)
                weights = weights * (1.0 / jnp.sum(weights, axis=0, keepdims=True))
                probs[i, :, lanes] = weights
                low = weights.astype(BF)
                part = mm(v_far_t[h * 64:h * 64 + 64], low[:KEYS]) + mm(v_loc_t[h * 64:h * 64 + 64], low[KEYS:])
                attn_t[i * 128 + h * 64:i * 128 + h * 64 + 64, p * 128:p * 128 + 128] = part.astype(BF)

    def chunk_of(terms, f):
        pieces = [terms[CHUNK * f:CHUNK * f + CHUNK, c * 128:c * 128 + 128] for c in range(3)]
        return jnp.concatenate(pieces + [jnp.zeros((8, 128), F32)], axis=0)

    landed_in(fg.at[1 - mp], mp_r.at[0])
    terms = mm(attn_t[...], fg[1 - core])
    for f in range(FAR):
        gw_x[f] = chunk_of(terms, f).astype(BF)
    send(gw_x, gw_pl, pair_s.at[3], pair_r.at[3], partner)

    attn = attn_t[...].T
    lo_send[...] = mm(attn, w_ref[:, pl.ds(pl.multiple_of((1 - mp) * 384, 128), 384)]).astype(BF)
    to_lo = pltpu.make_async_remote_copy(
        src_ref=lo_send, dst_ref=lo_land, send_sem=mp_s.at[1], recv_sem=mp_r.at[1],
        device_id=mp_id, device_id_type=MESH)
    to_lo.start()
    terms = mm(attn_t[...], fg[core])
    for f in range(FAR):
        gw_own[f] = chunk_of(terms, f)
    landed_in(gw_pl, pair_r.at[3])
    gw_send[...] = (gw_own[...] + gw_pl[...].astype(F32)).astype(BF)
    gw_land[hi] = gw_send[hi]
    for b in range(FAR_BITS):
        each(1 << b, hi, lambda j, b=b: send(
            gw_send.at[far_peer(b, j)], gw_land.at[hi], gw_s.at[0], gw_r.at[0], far_id(far_peer(b, j))))

    grad_attn = (mm_nt(fg[0], w_ref[:, 0:384]) + mm_nt(fg[1], w_ref[:, 384:768])).astype(BF)
    for i in range(3):
        lanes_i = slice(i * 128, i * 128 + 128)
        for p in range(2):
            part = grad_attn[p * 128:p * 128 + 128, lanes_i]
            for h in range(2):
                at = p * 256 + h * 128
                bdo[i, at:at + 128, :] = part * masks[h]
        gp_far = mm_nt(far[1, :, lanes_i], bdo[i])
        k_far_t = far[0, :, lanes_i].T
        d_scores, p_low = [], []
        for p in range(2):
            gp_loc = mm_nt(local_rows(v_ref, i, p, 1), bdo[i, p * 256:p * 256 + 256, :])
            k_loc_t = local_rows(k_ref, i, p, 0).T
            ds_half, pl_half = [], []
            for h in range(2):
                lanes = slice(p * 256 + h * 128, p * 256 + h * 128 + 128)
                weights = probs[i, :, lanes]
                grads = jnp.concatenate([gp_far[:, lanes], gp_loc[:, h * 128:h * 128 + 128]], axis=0)
                centre = jnp.sum(weights * grads, axis=0, keepdims=True)
                ds = (weights * (grads - centre) * HEAD ** -0.5).astype(BF)
                part = mm(k_far_t[h * 64:h * 64 + 64], ds[:KEYS]) + mm(k_loc_t[h * 64:h * 64 + 64], ds[KEYS:])
                dq_t[i * 128 + h * 64:i * 128 + h * 64 + 64, p * 128:p * 128 + 128] = part
                ds_half.append(ds)
                pl_half.append(weights.astype(BF))
            ds_p = jnp.concatenate(ds_half, axis=1)
            pl_p = jnp.concatenate(pl_half, axis=1)
            d_scores.append(ds_p)
            p_low.append(pl_p)
        for side, left, right in ((0, d_scores, bdq), (1, p_low, bdo)):
            grads = mm(jnp.concatenate([part[:KEYS] for part in left], axis=1), right[i])
            d_far[side, :, lanes_i] = grads
            d_x[side, :, lanes_i] = grads[64:KEYS].astype(BF)
            for p in range(2):
                grads = mm(left[p][KEYS:], right[i, p * 256:p * 256 + 256, :])
                d_loc[side, p * 128:p * 128 + 128, lanes_i] = grads[0:128]
                d_l1[side, 64 * (1 - p):64 * (1 - p) + 64, lanes_i] = grads[128:192].astype(BF)

    send(d_x.at[1 - core], d_land, pair_s.at[4], pair_r.at[4], partner)

    landed_in(d_land, pair_r.at[4])
    total = d_far[core, 64:KEYS, :] + d_land[...].astype(F32)
    d_send[...] = total[128:320].astype(BF)
    d_f32[...] = total[320:384]
    d_near[...] = total[0:128]
    each(8, hi, lambda j: send(
        d_f32.at[pl.ds(pl.multiple_of(j * 8, 8), 8)], r1_f32.at[pl.ds(pl.multiple_of(hi % 8 * 8, 8), 8)],
        r1_s.at[1], r1_r.at[1], far_id(far_peer(3, j))))
    for b in reversed(range(3)):
        r = BLOCK >> b
        each(1 << b, hi, lambda j, b=b, r=r: send(
            d_send.at[pl.ds(pl.multiple_of(b * BLOCK + j * r, 16), r)],
            r1_land.at[pl.ds(pl.multiple_of(b * BLOCK + hi % (1 << b) * r, 16), r)],
            r1_s.at[0], r1_r.at[0], far_id(far_peer(b, j))))

    landed_in(gw_land.at[pl.ds(0, FAR - 1)], gw_r.at[0])
    total = gw_land[0].astype(F32)
    for f in range(1, FAR):
        total = total + gw_land[f].astype(F32)
    gw_part[...] = total.astype(BF)
    gw_ar[depth] = gw_part[...]
    for t in range(1, 4):
        other = (depth + t) % 4
        send(gw_part, gw_ar.at[depth], gw_s.at[1], gw_r.at[1], near_id(other * 2 + core))

    landed_in(gw_ar.at[pl.ds(0, 3)], gw_r.at[1])
    total = gw_ar[0].astype(F32)
    for e in range(1, 4):
        total = total + gw_ar[e].astype(F32)
    gw_all[core, hi] = total.astype(BF)
    for b in range(FAR_BITS):
        each(1 << b, hi, lambda j, b=b: send(
            gw_all.at[core, hi], gw_all.at[core, hi], gw_s.at[2], gw_r.at[2 + b // 3], far_id(far_peer(b, j))))

    dq_out[...] = dq_t[...].T.astype(BF)
    stores[1].start()
    mine = mm(attn, w_ref[:, pl.ds(pl.multiple_of(mp * 384, 128), 384)])

    landed_in(r1_land, r1_r.at[0])
    landed_in(r1_f32, r1_r.at[1])
    landed = jnp.concatenate([r1_land[...], r1_f32[...].astype(BF)], axis=0)
    at_row, at_col = iota((64, 256), 0), iota((64, 256), 1)
    spread = jnp.zeros((64, 256), F32)
    for b in range(FAR_BITS):
        hit = (at_col // 64 == b) & (at_row // (1 << b) == at_col % (64 >> b))
        spread = jnp.where(hit, 0.5 ** b, spread)
    group_grad = mm(spread.astype(BF), landed).astype(BF)
    gg[core] = group_grad
    gg[1 - core] = jnp.zeros((64, 384), BF)
    at_row, at_col = iota((192, 64), 0), iota((192, 64), 1)
    spread = jnp.zeros((192, 64), F32)
    for b in range(NEAR_BITS):
        base = sibling(lo // (1 << b)) * (1 << b)
        hit = (at_row // 64 == b) & (at_col == 8 * base + at_row % 64 // (8 >> b))
        spread = jnp.where(hit, 0.5 ** (3 - b), spread)
    spread = mm(spread.astype(BF), group_grad)
    msg[...] = (d_near[...] + spread[64:192]).astype(BF)
    msg0[core] = (d_far[core, 0:64, :] + spread[0:64]).astype(BF)
    msg0[1 - core] = d_far[1 - core, 0:64, :].astype(BF)

    each(2, lo, lambda j: send(
        msg.at[pl.ds(pl.multiple_of(j * 32, 16), 32)], r2_land.at[core, pl.ds(64, 32)],
        r2_s.at[0], r2_r.at[0], near_id(near_peer(1, j))))
    each(4, lo, lambda j: send(
        msg.at[pl.ds(pl.multiple_of(64 + j * 16, 16), 16)],
        r2_land.at[core, pl.ds(pl.multiple_of(96 + depth % 2 * 16, 16), 16)],
        r2_s.at[0], r2_r.at[0], near_id(near_peer(2, j))))
    send(msg0, r2_land.at[:, pl.ds(0, 64)], pair_s.at[5], pair_r.at[5], partner)

    landed_in(gw_all.at[core, pl.ds(0, 7)], gw_r.at[2])
    eight = pl.multiple_of(hi // 8 * 8, 8)
    send(gw_all.at[core, pl.ds(eight, 8)], gw_all.at[core, pl.ds(eight, 8)], pair_s.at[6], pair_r.at[6], partner)
    landed_in(gw_all.at[core, pl.ds(0, 8)], gw_r.at[3])
    eight = pl.multiple_of(sibling(hi // 8) * 8, 8)
    send(gw_all.at[core, pl.ds(eight, 8)], gw_all.at[core, pl.ds(eight, 8)], pair_s.at[7], pair_r.at[7], partner)

    landed_in(r2_land.at[:, pl.ds(64, 64)], r2_r.at[0])
    landed_in(r2_land.at[:, pl.ds(0, 64)], pair_r.at[5])
    at_row, at_col = iota((256, 320), 0), iota((256, 320), 1)
    hits = (
        (at_col < 64) & (at_row // 4 == at_col),
        (at_col >= 64) & (at_col < 96) & (at_row // 8 == at_col - 64),
        (at_col >= 96) & (at_col < 128) & (at_row // 16 == at_col % 16),
        (at_col >= 128) & (at_col < 192) & (8 * lo + at_row // 32 == at_col - 128),
        (at_col >= 192) & (at_row // 2 == at_col - 192),
    )
    spread = jnp.zeros((256, 320), F32)
    for hit, weight in zip(hits, (0.25, 0.125, 0.0625, 0.03125, 0.5)):
        spread = jnp.where(hit, weight, spread)
    spread = spread.astype(BF)
    for side, out in ((0, dk_out), (1, dv_out)):
        terms = jnp.concatenate([r2_land[side], gg[side], d_l1[side]], axis=0)
        out[...] = (d_loc[side] + mm(spread, terms)).astype(BF)
        stores[2 + side].start()

    landed_in(lo_land, mp_r.at[1])
    lo_out[...] = (mine + lo_land[...].astype(F32)).astype(BF)
    stores[0].start()

    landed_in(gw_all.at[1 - core, pl.ds(0, 8)], pair_r.at[6])
    landed_in(gw_all.at[1 - core, pl.ds(0, 8)], pair_r.at[7])
    stores[4].start()

    landed_in(ug.at[pl.ds(0, NEAR - 1)], f1_s.at[0])
    landed_in(far.at[core, pl.ds(64, 128)], f1_s.at[1])
    landed_in(far.at[core, pl.ds(192, 192)], f2_s.at[0])
    landed_in(far_f32, f2_s.at[1])
    landed_in(r1_land, r1_s.at[0])
    landed_in(r1_f32, r1_s.at[1])
    landed_in(msg, r2_s.at[0])
    landed_in(gw_land.at[pl.ds(0, FAR - 1)], gw_s.at[0])
    landed_in(gw_ar.at[pl.ds(0, 3)], gw_s.at[1])
    landed_in(gw_land.at[pl.ds(0, FAR - 1)], gw_s.at[2])
    landed_in(msg0, pair_s.at[0])
    landed_in(msg, pair_s.at[1])
    landed_in(far.at[core, pl.ds(192, 256)], pair_s.at[2])
    landed_in(gw_x, pair_s.at[3])
    landed_in(d_land, pair_s.at[4])
    landed_in(msg0, pair_s.at[5])
    landed_in(gw_all.at[core, pl.ds(0, 8)], pair_s.at[6])
    landed_in(gw_all.at[core, pl.ds(0, 8)], pair_s.at[7])
    to_mp.wait_send()
    to_lo.wait_send()
    for store in stores:
        store.wait()


def hand_over(*refs):
    given, out, held, whole, sem = refs[0:5], refs[5:10], refs[10:15], refs[15], refs[16]
    first = [pltpu.make_async_copy(given[n], held[n], sem.at[n]) for n in range(5)]
    second = [pltpu.make_async_copy(held[n], out[n], sem.at[5 + n]) for n in range(4)]
    second.append(pltpu.make_async_copy(whole, out[4], sem.at[9]))
    for n in (4, 0, 1, 2, 3):
        first[n].start()
    first[4].wait()
    for side in range(2):
        for f in range(FAR):
            part = held[4][side, f].astype(F32)
            for c in range(3):
                at = side * 384 + c * 128
                whole[CHUNK * f:CHUNK * f + CHUNK, at:at + 128] = part[c * CHUNK:c * CHUNK + CHUNK]
    second[4].start()
    for n in range(4):
        first[n].wait()
        second[n].start()
    for copy in second:
        copy.wait()


def on_device(query_rows, key_rows, value_rows, w_output, grad_output):
    vm = pltpu.VMEM
    dma = pltpu.SemaphoreType.DMA
    piece = (80, 128)
    scratch = [
        vm((256, 384), BF), vm((256, 384), BF), vm((256, 384), BF), vm((256, 384), BF),
        vm((256, 384), BF), vm((256, 384), BF), vm((256, 384), BF), vm((384, 768), BF), vm((256, 384), BF),
        vm((2, 128, 384), BF),
        vm((2, 128, 384), BF),
        vm((2, KEYS, 384), BF),
        vm((64, 384), F32),
        vm((NEAR, 16, 384), BF),
        vm((112, 384), BF),
        vm((8, 384), F32),
        vm((2, 256, 384), BF),
        vm((3, 512, 128), BF),
        vm((3, 512, 128), BF),
        vm((3, KEYS + 192, 512), F32),
        vm((384, 256), BF),
        vm((384, 256), F32),
        vm((2, KEYS, 384), F32),
        vm((2, 384, 384), BF),
        vm((384, 384), BF),
        vm((128, 384), F32),
        vm((192, 384), BF),
        vm((64, 384), F32),
        vm((192, 384), BF),
        vm((64, 384), F32),
        vm((2, 64, 384), BF),
        vm((2, 64, 384), BF),
        vm((128, 384), BF),
        vm((2, 128, 384), BF),
        vm((2, 256, 384), F32),
        vm((2, 128, 384), BF),
        vm((FAR,) + piece, BF),
        vm((FAR,) + piece, BF),
        vm((FAR,) + piece, F32),
        vm((FAR,) + piece, BF),
        vm((FAR,) + piece, BF),
        vm(piece, BF),
        vm((4,) + piece, BF),
        vm((2, FAR) + piece, BF),
        vm((256, 384), BF),
        vm((256, 384), BF),
        dma((5,)),
        dma((5,)),
        dma((2,)), dma((2,)),
        dma((2,)), dma((2,)),
        dma((2,)), dma((2,)),
        dma((1,)), dma((1,)),
        dma((3,)), dma((4,)),
        dma((8,)), dma((8,)),
        dma((2,)), dma((2,)),
    ]
    rows = jax.ShapeDtypeStruct((256, 384), BF)
    chunks = jax.ShapeDtypeStruct((2, FAR) + piece, BF)
    in_hbm = pl.BlockSpec(memory_space=pltpu.HBM)
    results = pl.pallas_call(
        kernel,
        out_shape=(rows, rows, rows, rows, chunks),
        in_specs=[in_hbm] * 5,
        out_specs=(in_hbm,) * 5,
        scratch_shapes=scratch,
        compiler_params=pltpu.CompilerParams(
            collective_id=0, has_side_effects=True, vmem_limit_bytes=58 * 1024 * 1024),
        cost_estimate=pl.CostEstimate(flops=1_200_000_000, bytes_accessed=4_000_000, transcendentals=1_000_000),
    )(query_rows, key_rows, value_rows, w_output, grad_output)
    held = [vm((256, 384), BF)] * 4 + [vm((2, FAR) + piece, BF), vm((384, 768), F32)]
    return pl.pallas_call(
        hand_over,
        out_shape=(rows, rows, rows, rows, jax.ShapeDtypeStruct((384, 768), F32)),
        in_specs=[in_hbm] * 5,
        out_specs=(in_hbm,) * 5,
        scratch_shapes=held + [dma((10,))],
        compiler_params=pltpu.CompilerParams(vmem_limit_bytes=58 * 1024 * 1024),
    )(*results)


def solution(mesh):
    placed = (P("ctx", "mp"), P("ctx", "mp"), P("ctx", "mp"), P("mp", None), P("ctx", "mp"))
    return jax.shard_map(
        on_device,
        mesh=mesh,
        in_specs=placed,
        out_specs=(P("ctx", "mp"), P("ctx", "mp"), P("ctx", "mp"), P("ctx", "mp"), P("mp", None)),
        check_vma=False,
    )
```

time: 70.1 us -> 53.6 us (0.76); the launches traced: 68.9 us -> 53.5 us
  local copies, waits for them, and re-layouts: 8.48 us -> 0 us
  Pallas kernels: 59.8 us -> 52.8 us
    unnamed x15 -> x0, local copies, waits for them, and re-layouts: 8.48 us -> none
    pallas_call x1 -> x2, Pallas kernels: 59.8 us -> 52.8 us  [the longest x1 50.3 us: on_device(): pl.pallas_call(kernel, out_shape=(rows, rows, rows, rows, chunks), in_spe...]
where the time goes in v2:
time: 53.6 us; the launch traced here: 53.5 us
  Pallas kernels  52.8 us (99%)
  between operations  0.64 us (1%)
    pallas_call x1, Pallas kernels, on_device(): pl.pallas_call(kernel, out_shape=(rows, rows, rows, rows, chunks), in_spe...  50.3 us
    pallas_call x1, Pallas kernels, on_device(): pl.pallas_call(hand_over, out_shape=(rows, rows, rows, rows, jax.ShapeDty...  2.51 us

profile of v2, /device:TPU:1, one launch (start us, length us, event | category | flops | bytes accessed | tf_op | source)
XLA Modules:
  0.0 53.5 jit_solution(11189039858285619197)
XLA Ops:
  0.6 50.3 %shard_map.92 = (bf16[256,384]{1,0:T(8,128)(2,1)}, bf16[256,384]{1,0:T(8,128)(2,1)}, bf16[256,384]{1,0:T(8,128)(2,1)}, bf16[256,384]{1,0:T(8,128)(2,1)}, bf16[2,16,80,128]{3,2,1,0:T(8,128)(2,1)}) custom-call(bf16[256,384]{1,0:T(8,128)(2,1)} %q_hbm.1, bf16[256,384]{1,0:T(8,128)(2,1)} %k_hbm.1, bf16[256,384]{1,0:T(8,128)(2,1)} %v_hbm.1, ...), custom_call_target="tpu_custom_call" | custom-call | flops 1200000000 | bytes 4000000 | tf_op jit(solution)/shard_map/pallas_call | solution.py:500
  50.9 2.5 %shard_map.93 = (bf16[256,384]{1,0:T(8,128)(2,1)}, bf16[256,384]{1,0:T(8,128)(2,1)}, bf16[256,384]{1,0:T(8,128)(2,1)}, bf16[256,384]{1,0:T(8,128)(2,1)}, f32[384,768]{1,0:T(8,128)}) custom-call(bf16[256,384]{1,0:T(8,128)(2,1)} %get-tuple-element.10.refs_0_, bf16[256,384]{1,0:T(8,128)(2,1)} %get-tuple-element.11.refs_1_, ...), custom_call_target="tpu_custom_call" | custom-call | tf_op jit(solution)/shard_map/pallas_call | solution.py:511

commit v3 on v2

--- a/solution.py
+++ b/solution.py
@@ -34,13 +34,6 @@
     return lax.dot_general(a, b, (((1,), (1,)), ((), ())), preferred_element_type=F32)
 
 
-def pool(rows):
-    count = rows.shape[0]
-    out = max(count // 2, 16)
-    halves = where_one(iota((out, count), 1) // 2 == iota((out, count), 0), 0.5)
-    return mm(halves, rows).astype(BF)
-
-
 def sibling(index):
     return index + 1 - 2 * (index % 2)
 
@@ -50,7 +43,7 @@
     lo_hbm, dq_hbm, dk_hbm, dv_hbm, gw_hbm,
     lo_out, dq_out, dk_out, dv_out,
     q_ref, k_ref, v_ref, w_ref, go_ref,
-    near_rows, level1, far, far_f32, ug, up, up_f32, fg, bdq, bdo, probs, attn_t, dq_t,
+    steps_ref, upper_ref, to_group, to_near, to_rows, k_loc_t, v_loc_t, near_rows, level1, far, far_f32, ug, up, up_f32, fg, bdq, bdo, probs, attn_t, dq_t,
     d_far, d_x, d_land, d_near, d_send, d_f32, r1_land, r1_f32, gg, msg0, msg, r2_land, d_loc, d_l1,
     gw_x, gw_pl, gw_own, gw_send, gw_land, gw_part, gw_ar, gw_all, lo_send, lo_land,
     ld, st, f1_s, f1_r, f2_s, f2_r, r1_s, r1_r, r2_s, r2_r, gw_s, gw_r, pair_s, pair_r, mp_s, mp_r,
@@ -110,31 +103,33 @@
 
     loads[0].wait()
     loads[1].wait()
-    rows = jnp.concatenate([k_ref[...], v_ref[...]], axis=1)
-
-    def keep(ref, start, rows):
-        for side in range(2):
-            ref[side, start:start + rows.shape[0], :] = rows[:, side * 384:side * 384 + 384]
-
-    rows = pool(rows)
-    keep(level1, 0, rows)
-    rows = pool(rows)
-    keep(near_rows, 0, rows)
-    rows = pool(rows)
-    keep(near_rows, 64, rows)
-    rows = pool(rows)
-    keep(near_rows, 96, rows)
-    first = pool(rows)
-    step_up = where_one(iota((16, 16), 1) // 2 + 8 == iota((16, 16), 0), 0.5)
-    upper = first
-    for _ in range(3):
-        upper = (first.astype(F32) + mm(step_up, upper)).astype(BF)
-    keep(near_rows, 112, upper)
+    for side, own in ((0, k_ref), (1, v_ref)):
+        kept = ((level1, 0), (near_rows, 0), (near_rows, 64), (near_rows, 96))
+        for c in range(3):
+            lanes = slice(c * 128, c * 128 + 128)
+            steps, upper = steps_ref.at[3 * side + c], upper_ref.at[3 * side + c]
+            steps[...] = own[:, lanes].astype(F32)
+            count = 256
+            for level in range(8):
+                count //= 2
+                rows = (steps[pl.ds(0, count, stride=2), :] + steps[pl.ds(1, count, stride=2), :]) * 0.5
+                low = rows.astype(BF)
+                rows = low.astype(F32)
+                if level < 4:
+                    ref, start = kept[level]
+                    ref[side, start:start + count, lanes] = low
+                else:
+                    at = (0, 8, 12, 14)[level - 4]
+                    upper[at:at + count, :] = rows
+                if level < 7:
+                    steps[0:count, :] = rows
+            upper[15:16, :] = jnp.zeros((1, 128), F32)
+            near_rows[side, 112:128, lanes] = upper[...].astype(BF)
     ug[lo] = near_rows[core, 112:128, :]
 
     pl.semaphore_wait(barrier, NEAR - 1 + FAR - 1 + 1)
 
-    for b in range(NEAR_BITS):
+    for b in reversed(range(NEAR_BITS)):
         each(1 << b, lo, lambda j, b=b: send(
             near_rows.at[near_peer(b, j) % 2, pl.ds(112, 16)], ug.at[lo], f1_s.at[0], f1_r.at[0],
             near_id(near_peer(b, j))))
@@ -148,6 +143,7 @@
     partner = near_id(sibling(lo))
     send(near_rows.at[:, pl.ds(0, 64)], far.at[:, pl.ds(0, 64)], pair_s.at[0], pair_r.at[0], partner)
 
+
     lane_low = iota((128, 128), 1) < HEAD
     masks = (where_one(lane_low, 1.0), where_one(jnp.logical_not(lane_low), 1.0))
 
@@ -195,6 +191,41 @@
     to_mp.start()
     fg[mp] = go_ref[...]
 
+    for i in range(3):
+        for p in range(2):
+            k_loc_t[i, p] = local_rows(k_ref, i, p, 0).T
+            v_loc_t[i, p] = local_rows(v_ref, i, p, 1).T
+
+    at_row, at_col = iota((64, 256), 0), iota((64, 256), 1)
+    spread = jnp.zeros((64, 256), F32)
+    for b in range(FAR_BITS):
+        hit = (at_col // 64 == b) & (at_row // (1 << b) == at_col % (64 >> b))
+        spread = jnp.where(hit, 0.5 ** b, spread)
+    to_group[...] = spread.astype(BF)
+    at_row, at_col = iota((192, 64), 0), iota((192, 64), 1)
+    spread = jnp.zeros((192, 64), F32)
+    for b in range(NEAR_BITS):
+        base = sibling(lo // (1 << b)) * (1 << b)
+        hit = (at_row // 64 == b) & (at_col == 8 * base + at_row % 64 // (8 >> b))
+        spread = jnp.where(hit, 0.5 ** (3 - b), spread)
+    to_near[...] = spread.astype(BF)
+    at_row, at_col = iota((256, 320), 0), iota((256, 320), 1)
+    hits = (
+        (at_col < 64) & (at_row // 4 == at_col),
+        (at_col >= 64) & (at_col < 96) & (at_row // 8 == at_col - 64),
+        (at_col >= 96) & (at_col < 128) & (at_row // 16 == at_col % 16),
+        (at_col >= 128) & (at_col < 192) & (8 * lo + at_row // 32 == at_col - 128),
+        (at_col >= 192) & (at_row // 2 == at_col - 192),
+    )
+    spread = jnp.zeros((256, 320), F32)
+    for hit, weight in zip(hits, (0.25, 0.125, 0.0625, 0.03125, 0.5)):
+        spread = jnp.where(hit, weight, spread)
+    to_rows[...] = spread.astype(BF)
+
+    landed_in(far_f32, f2_r.at[1])
+    far[core, 384:448, :] = far_f32[...].astype(BF)
+    landed_in(far.at[core, pl.ds(192, 192)], f2_r.at[0])
+    send(far.at[core, pl.ds(192, 256)], far.at[core, pl.ds(192, 256)], pair_s.at[2], pair_r.at[2], partner)
     landed_in(far.at[core, pl.ds(64, 128)], f1_r.at[1])
     send(far.at[core, pl.ds(64, 128)], far.at[core, pl.ds(64, 128)], pair_s.at[1], pair_r.at[1], partner)
     landed_in(far.at[:, pl.ds(0, 64)], pair_r.at[0])
@@ -202,10 +233,6 @@
     for i in range(3):
         probs[i, 0:192, :] = mm_nt(far[0, 0:192, i * 128:i * 128 + 128], bdq[i])
 
-    landed_in(far_f32, f2_r.at[1])
-    far[core, 384:448, :] = far_f32[...].astype(BF)
-    landed_in(far.at[core, pl.ds(192, 192)], f2_r.at[0])
-    send(far.at[core, pl.ds(192, 256)], far.at[core, pl.ds(192, 256)], pair_s.at[2], pair_r.at[2], partner)
     landed_in(far.at[1 - core, pl.ds(192, 256)], pair_r.at[2])
 
     unit = HEAD ** -0.5 * 1.4426950408889634
@@ -213,7 +240,6 @@
         probs[i, 192:KEYS, :] = mm_nt(far[0, 192:KEYS, i * 128:i * 128 + 128], bdq[i])
         v_far_t = far[1, :, i * 128:i * 128 + 128].T
         for p in range(2):
-            v_loc_t = local_rows(v_ref, i, p, 1).T
             for h in range(2):
                 lanes = slice(p * 256 + h * 128, p * 256 + h * 128 + 128)
                 scores = probs[i, :, lanes] * unit
@@ -222,18 +248,8 @@
                 weights = weights * (1.0 / jnp.sum(weights, axis=0, keepdims=True))
                 probs[i, :, lanes] = weights
                 low = weights.astype(BF)
-                part = mm(v_far_t[h * 64:h * 64 + 64], low[:KEYS]) + mm(v_loc_t[h * 64:h * 64 + 64], low[KEYS:])
+                part = mm(v_far_t[h * 64:h * 64 + 64], low[:KEYS]) + mm(v_loc_t[i, p, h * 64:h * 64 + 64], low[KEYS:])
                 attn_t[i * 128 + h * 64:i * 128 + h * 64 + 64, p * 128:p * 128 + 128] = part.astype(BF)
-
-    def chunk_of(terms, f):
-        pieces = [terms[CHUNK * f:CHUNK * f + CHUNK, c * 128:c * 128 + 128] for c in range(3)]
-        return jnp.concatenate(pieces + [jnp.zeros((8, 128), F32)], axis=0)
-
-    landed_in(fg.at[1 - mp], mp_r.at[0])
-    terms = mm(attn_t[...], fg[1 - core])
-    for f in range(FAR):
-        gw_x[f] = chunk_of(terms, f).astype(BF)
-    send(gw_x, gw_pl, pair_s.at[3], pair_r.at[3], partner)
 
     attn = attn_t[...].T
     lo_send[...] = mm(attn, w_ref[:, pl.ds(pl.multiple_of((1 - mp) * 384, 128), 384)]).astype(BF)
@@ -241,13 +257,24 @@
         src_ref=lo_send, dst_ref=lo_land, send_sem=mp_s.at[1], recv_sem=mp_r.at[1],
         device_id=mp_id, device_id_type=MESH)
     to_lo.start()
+
+    def chunk_of(terms, f):
+        pieces = [terms[CHUNK * f:CHUNK * f + CHUNK, c * 128:c * 128 + 128] for c in range(3)]
+        return jnp.concatenate(pieces + [jnp.zeros((8, 128), F32)], axis=0)
+
+    landed_in(fg.at[1 - mp], mp_r.at[0])
+    terms = mm(attn_t[...], fg[1 - core])
+    for f in range(FAR):
+        gw_x[f] = chunk_of(terms, f).astype(BF)
+    send(gw_x, gw_pl, pair_s.at[3], pair_r.at[3], partner)
+
     terms = mm(attn_t[...], fg[core])
     for f in range(FAR):
         gw_own[f] = chunk_of(terms, f)
     landed_in(gw_pl, pair_r.at[3])
     gw_send[...] = (gw_own[...] + gw_pl[...].astype(F32)).astype(BF)
     gw_land[hi] = gw_send[hi]
-    for b in range(FAR_BITS):
+    for b in reversed(range(FAR_BITS)):
         each(1 << b, hi, lambda j, b=b: send(
             gw_send.at[far_peer(b, j)], gw_land.at[hi], gw_s.at[0], gw_r.at[0], far_id(far_peer(b, j))))
 
@@ -259,12 +286,13 @@
             for h in range(2):
                 at = p * 256 + h * 128
                 bdo[i, at:at + 128, :] = part * masks[h]
+    for i in range(3):
+        lanes_i = slice(i * 128, i * 128 + 128)
         gp_far = mm_nt(far[1, :, lanes_i], bdo[i])
         k_far_t = far[0, :, lanes_i].T
         d_scores, p_low = [], []
         for p in range(2):
             gp_loc = mm_nt(local_rows(v_ref, i, p, 1), bdo[i, p * 256:p * 256 + 256, :])
-            k_loc_t = local_rows(k_ref, i, p, 0).T
             ds_half, pl_half = [], []
             for h in range(2):
                 lanes = slice(p * 256 + h * 128, p * 256 + h * 128 + 128)
@@ -272,7 +300,7 @@
                 grads = jnp.concatenate([gp_far[:, lanes], gp_loc[:, h * 128:h * 128 + 128]], axis=0)
                 centre = jnp.sum(weights * grads, axis=0, keepdims=True)
                 ds = (weights * (grads - centre) * HEAD ** -0.5).astype(BF)
-                part = mm(k_far_t[h * 64:h * 64 + 64], ds[:KEYS]) + mm(k_loc_t[h * 64:h * 64 + 64], ds[KEYS:])
+                part = mm(k_far_t[h * 64:h * 64 + 64], ds[:KEYS]) + mm(k_loc_t[i, p, h * 64:h * 64 + 64], ds[KEYS:])
                 dq_t[i * 128 + h * 64:i * 128 + h * 64 + 64, p * 128:p * 128 + 128] = part
                 ds_half.append(ds)
                 pl_half.append(weights.astype(BF))
@@ -291,6 +319,16 @@
 
     send(d_x.at[1 - core], d_land, pair_s.at[4], pair_r.at[4], partner)
 
+    landed_in(gw_land.at[pl.ds(0, FAR - 1)], gw_r.at[0])
+    total = gw_land[0].astype(F32)
+    for f in range(1, FAR):
+        total = total + gw_land[f].astype(F32)
+    gw_part[...] = total.astype(BF)
+    gw_ar[depth] = gw_part[...]
+    for t in range(1, 4):
+        other = (depth + t) % 4
+        send(gw_part, gw_ar.at[depth], gw_s.at[1], gw_r.at[1], near_id(other * 2 + core))
+
     landed_in(d_land, pair_r.at[4])
     total = d_far[core, 64:KEYS, :] + d_land[...].astype(F32)
     d_send[...] = total[128:320].astype(BF)
@@ -306,16 +344,6 @@
             r1_land.at[pl.ds(pl.multiple_of(b * BLOCK + hi % (1 << b) * r, 16), r)],
             r1_s.at[0], r1_r.at[0], far_id(far_peer(b, j))))
 
-    landed_in(gw_land.at[pl.ds(0, FAR - 1)], gw_r.at[0])
-    total = gw_land[0].astype(F32)
-    for f in range(1, FAR):
-        total = total + gw_land[f].astype(F32)
-    gw_part[...] = total.astype(BF)
-    gw_ar[depth] = gw_part[...]
-    for t in range(1, 4):
-        other = (depth + t) % 4
-        send(gw_part, gw_ar.at[depth], gw_s.at[1], gw_r.at[1], near_id(other * 2 + core))
-
     landed_in(gw_ar.at[pl.ds(0, 3)], gw_r.at[1])
     total = gw_ar[0].astype(F32)
     for e in range(1, 4):
@@ -332,21 +360,10 @@
     landed_in(r1_land, r1_r.at[0])
     landed_in(r1_f32, r1_r.at[1])
     landed = jnp.concatenate([r1_land[...], r1_f32[...].astype(BF)], axis=0)
-    at_row, at_col = iota((64, 256), 0), iota((64, 256), 1)
-    spread = jnp.zeros((64, 256), F32)
-    for b in range(FAR_BITS):
-        hit = (at_col // 64 == b) & (at_row // (1 << b) == at_col % (64 >> b))
-        spread = jnp.where(hit, 0.5 ** b, spread)
-    group_grad = mm(spread.astype(BF), landed).astype(BF)
+    group_grad = mm(to_group[...], landed).astype(BF)
     gg[core] = group_grad
     gg[1 - core] = jnp.zeros((64, 384), BF)
-    at_row, at_col = iota((192, 64), 0), iota((192, 64), 1)
-    spread = jnp.zeros((192, 64), F32)
-    for b in range(NEAR_BITS):
-        base = sibling(lo // (1 << b)) * (1 << b)
-        hit = (at_row // 64 == b) & (at_col == 8 * base + at_row % 64 // (8 >> b))
-        spread = jnp.where(hit, 0.5 ** (3 - b), spread)
-    spread = mm(spread.astype(BF), group_grad)
+    spread = mm(to_near[...], group_grad)
     msg[...] = (d_near[...] + spread[64:192]).astype(BF)
     msg0[core] = (d_far[core, 0:64, :] + spread[0:64]).astype(BF)
     msg0[1 - core] = d_far[1 - core, 0:64, :].astype(BF)
@@ -369,21 +386,9 @@
 
     landed_in(r2_land.at[:, pl.ds(64, 64)], r2_r.at[0])
     landed_in(r2_land.at[:, pl.ds(0, 64)], pair_r.at[5])
-    at_row, at_col = iota((256, 320), 0), iota((256, 320), 1)
-    hits = (
-        (at_col < 64) & (at_row // 4 == at_col),
-        (at_col >= 64) & (at_col < 96) & (at_row // 8 == at_col - 64),
-        (at_col >= 96) & (at_col < 128) & (at_row // 16 == at_col % 16),
-        (at_col >= 128) & (at_col < 192) & (8 * lo + at_row // 32 == at_col - 128),
-        (at_col >= 192) & (at_row // 2 == at_col - 192),
-    )
-    spread = jnp.zeros((256, 320), F32)
-    for hit, weight in zip(hits, (0.25, 0.125, 0.0625, 0.03125, 0.5)):
-        spread = jnp.where(hit, weight, spread)
-    spread = spread.astype(BF)
     for side, out in ((0, dk_out), (1, dv_out)):
         terms = jnp.concatenate([r2_land[side], gg[side], d_l1[side]], axis=0)
-        out[...] = (d_loc[side] + mm(spread, terms)).astype(BF)
+        out[...] = (d_loc[side] + mm(to_rows[...], terms)).astype(BF)
         stores[2 + side].start()
 
     landed_in(lo_land, mp_r.at[1])
@@ -420,19 +425,21 @@
 
 def hand_over(*refs):
     given, out, held, whole, sem = refs[0:5], refs[5:10], refs[10:15], refs[15], refs[16]
-    first = [pltpu.make_async_copy(given[n], held[n], sem.at[n]) for n in range(5)]
-    second = [pltpu.make_async_copy(held[n], out[n], sem.at[5 + n]) for n in range(4)]
-    second.append(pltpu.make_async_copy(whole, out[4], sem.at[9]))
-    for n in (4, 0, 1, 2, 3):
-        first[n].start()
-    first[4].wait()
+    first = [pltpu.make_async_copy(given[n], held[n], sem.at[n]) for n in range(4)]
+    halves = [pltpu.make_async_copy(given[4].at[n], held[4].at[n], sem.at[8 + n]) for n in range(2)]
+    second = [pltpu.make_async_copy(held[n], out[n], sem.at[4 + n]) for n in range(4)]
+    for copy in halves + first:
+        copy.start()
     for side in range(2):
+        halves[side].wait()
         for f in range(FAR):
             part = held[4][side, f].astype(F32)
             for c in range(3):
                 at = side * 384 + c * 128
                 whole[CHUNK * f:CHUNK * f + CHUNK, at:at + 128] = part[c * CHUNK:c * CHUNK + CHUNK]
-    second[4].start()
+        columns = pl.ds(side * 384, 384)
+        second.append(pltpu.make_async_copy(whole.at[:, columns], out[4].at[:, columns], sem.at[10 + side]))
+        second[-1].start()
     for n in range(4):
         first[n].wait()
         second[n].start()
@@ -447,6 +454,13 @@
     scratch = [
         vm((256, 384), BF), vm((256, 384), BF), vm((256, 384), BF), vm((256, 384), BF),
         vm((256, 384), BF), vm((256, 384), BF), vm((256, 384), BF), vm((384, 768), BF), vm((256, 384), BF),
+        vm((6, 256, 128), F32),
+        vm((6, 16, 128), F32),
+        vm((64, 256), BF),
+        vm((192, 64), BF),
+        vm((256, 320), BF),
+        vm((3, 2, 128, 192), BF),
+        vm((3, 2, 128, 192), BF),
         vm((2, 128, 384), BF),
         vm((2, 128, 384), BF),
         vm((2, KEYS, 384), BF),
@@ -513,7 +527,7 @@
         out_shape=(rows, rows, rows, rows, jax.ShapeDtypeStruct((384, 768), F32)),
         in_specs=[in_hbm] * 5,
         out_specs=(in_hbm,) * 5,
-        scratch_shapes=held + [dma((10,))],
+        scratch_shapes=held + [dma((12,))],
         compiler_params=pltpu.CompilerParams(vmem_limit_bytes=58 * 1024 * 1024),
     )(*results)
 

time: 53.6 us -> 52.7 us (0.983)
  Pallas kernels: 52.8 us -> 52 us
    pallas_call x1, Pallas kernels: 50.3 us -> 49.6 us  [on_device(): pl.pallas_call(kernel, out_shape=(rows, rows, rows, rows, chunks), in_spe...]
where the time goes in v3:
time: 52.7 us; the launch traced here: 52.6 us
  Pallas kernels  52 us (99%)
  between operations  0.64 us (1%)
    pallas_call x1, Pallas kernels, on_device(): pl.pallas_call(kernel, out_shape=(rows, rows, rows, rows, chunks), in_spe...  49.6 us
    pallas_call x1, Pallas kernels, on_device(): pl.pallas_call(hand_over, out_shape=(rows, rows, rows, rows, jax.ShapeDty...  2.38 us

profile of v3, /device:TPU:1, one launch (start us, length us, event | category | flops | bytes accessed | tf_op | source)
XLA Modules:
  0.0 52.6 jit_solution(8113566949366116439)
XLA Ops:
  0.6 49.6 %shard_map.92 = (bf16[256,384]{1,0:T(8,128)(2,1)}, bf16[256,384]{1,0:T(8,128)(2,1)}, bf16[256,384]{1,0:T(8,128)(2,1)}, bf16[256,384]{1,0:T(8,128)(2,1)}, bf16[2,16,80,128]{3,2,1,0:T(8,128)(2,1)}) custom-call(bf16[256,384]{1,0:T(8,128)(2,1)} %q_hbm.1, bf16[256,384]{1,0:T(8,128)(2,1)} %k_hbm.1, bf16[256,384]{1,0:T(8,128)(2,1)} %v_hbm.1, ...), custom_call_target="tpu_custom_call" | custom-call | flops 1200000000 | bytes 4000000 | tf_op jit(solution)/shard_map/pallas_call | solution.py:514
  50.2 2.4 %shard_map.93 = (bf16[256,384]{1,0:T(8,128)(2,1)}, bf16[256,384]{1,0:T(8,128)(2,1)}, bf16[256,384]{1,0:T(8,128)(2,1)}, bf16[256,384]{1,0:T(8,128)(2,1)}, f32[384,768]{1,0:T(8,128)}) custom-call(bf16[256,384]{1,0:T(8,128)(2,1)} %get-tuple-element.10.refs_0_, bf16[256,384]{1,0:T(8,128)(2,1)} %get-tuple-element.11.refs_1_, ...), custom_call_target="tpu_custom_call" | custom-call | tf_op jit(solution)/shard_map/pallas_call | solution.py:525

commit v4 on v3

--- a/solution.py
+++ b/solution.py
@@ -43,7 +43,7 @@
     lo_hbm, dq_hbm, dk_hbm, dv_hbm, gw_hbm,
     lo_out, dq_out, dk_out, dv_out,
     q_ref, k_ref, v_ref, w_ref, go_ref,
-    steps_ref, upper_ref, to_group, to_near, to_rows, k_loc_t, v_loc_t, near_rows, level1, far, far_f32, ug, up, up_f32, fg, bdq, bdo, probs, attn_t, dq_t,
+    steps_ref, upper_ref, k_far_t, to_group, to_near, to_rows, k_loc_t, v_loc_t, near_rows, level1, far, far_f32, ug, up, up_f32, fg, bdq, bdo, probs, attn_t, dq_t,
     d_far, d_x, d_land, d_near, d_send, d_f32, r1_land, r1_f32, gg, msg0, msg, r2_land, d_loc, d_l1,
     gw_x, gw_pl, gw_own, gw_send, gw_land, gw_part, gw_ar, gw_all, lo_send, lo_land,
     ld, st, f1_s, f1_r, f2_s, f2_r, r1_s, r1_r, r2_s, r2_r, gw_s, gw_r, pair_s, pair_r, mp_s, mp_r,
@@ -74,7 +74,7 @@
         return sibling(hi // (1 << b)) * (1 << b) + j
 
     def each(n, mine, body):
-        if n <= 2:
+        if n <= 8:
             for j in range(n):
                 body((j + mine) % n)
         else:
@@ -262,6 +262,8 @@
         pieces = [terms[CHUNK * f:CHUNK * f + CHUNK, c * 128:c * 128 + 128] for c in range(3)]
         return jnp.concatenate(pieces + [jnp.zeros((8, 128), F32)], axis=0)
 
+    for i in range(3):
+        k_far_t[i] = far[0, :, i * 128:i * 128 + 128].T
     landed_in(fg.at[1 - mp], mp_r.at[0])
     terms = mm(attn_t[...], fg[1 - core])
     for f in range(FAR):
@@ -289,7 +291,6 @@
     for i in range(3):
         lanes_i = slice(i * 128, i * 128 + 128)
         gp_far = mm_nt(far[1, :, lanes_i], bdo[i])
-        k_far_t = far[0, :, lanes_i].T
         d_scores, p_low = [], []
         for p in range(2):
             gp_loc = mm_nt(local_rows(v_ref, i, p, 1), bdo[i, p * 256:p * 256 + 256, :])
@@ -300,7 +301,7 @@
                 grads = jnp.concatenate([gp_far[:, lanes], gp_loc[:, h * 128:h * 128 + 128]], axis=0)
                 centre = jnp.sum(weights * grads, axis=0, keepdims=True)
                 ds = (weights * (grads - centre) * HEAD ** -0.5).astype(BF)
-                part = mm(k_far_t[h * 64:h * 64 + 64], ds[:KEYS]) + mm(k_loc_t[i, p, h * 64:h * 64 + 64], ds[KEYS:])
+                part = mm(k_far_t[i, h * 64:h * 64 + 64], ds[:KEYS]) + mm(k_loc_t[i, p, h * 64:h * 64 + 64], ds[KEYS:])
                 dq_t[i * 128 + h * 64:i * 128 + h * 64 + 64, p * 128:p * 128 + 128] = part
                 ds_half.append(ds)
                 pl_half.append(weights.astype(BF))
@@ -456,6 +457,7 @@
         vm((256, 384), BF), vm((256, 384), BF), vm((256, 384), BF), vm((384, 768), BF), vm((256, 384), BF),
         vm((6, 256, 128), F32),
         vm((6, 16, 128), F32),
+        vm((3, 128, KEYS), BF),
         vm((64, 256), BF),
         vm((192, 64), BF),
         vm((256, 320), BF),

time: 52.7 us -> 52.4 us (level)
  no operation moved by 1% of the time
where the time goes in v4:
time: 52.4 us; the launch traced here: 52.3 us
  Pallas kernels  51.6 us (98%)
  between operations  0.64 us (1%)
    pallas_call x1, Pallas kernels, on_device(): pl.pallas_call(kernel, out_shape=(rows, rows, rows, rows, chunks), in_spe...  49.2 us
    pallas_call x1, Pallas kernels, on_device(): pl.pallas_call(hand_over, out_shape=(rows, rows, rows, rows, jax.ShapeDty...  2.38 us

profile of v4, /device:TPU:1, one launch (start us, length us, event | category | flops | bytes accessed | tf_op | source)
XLA Modules:
  0.0 52.3 jit_solution(12859109327127266072)
XLA Ops:
  0.6 49.2 %shard_map.92 = (bf16[256,384]{1,0:T(8,128)(2,1)}, bf16[256,384]{1,0:T(8,128)(2,1)}, bf16[256,384]{1,0:T(8,128)(2,1)}, bf16[256,384]{1,0:T(8,128)(2,1)}, bf16[2,16,80,128]{3,2,1,0:T(8,128)(2,1)}) custom-call(bf16[256,384]{1,0:T(8,128)(2,1)} %q_hbm.1, bf16[256,384]{1,0:T(8,128)(2,1)} %k_hbm.1, bf16[256,384]{1,0:T(8,128)(2,1)} %v_hbm.1, ...), custom_call_target="tpu_custom_call" | custom-call | flops 1200000000 | bytes 4000000 | tf_op jit(solution)/shard_map/pallas_call | solution.py:516
  49.9 2.4 %shard_map.93 = (bf16[256,384]{1,0:T(8,128)(2,1)}, bf16[256,384]{1,0:T(8,128)(2,1)}, bf16[256,384]{1,0:T(8,128)(2,1)}, bf16[256,384]{1,0:T(8,128)(2,1)}, f32[384,768]{1,0:T(8,128)}) custom-call(bf16[256,384]{1,0:T(8,128)(2,1)} %get-tuple-element.10.refs_0_, bf16[256,384]{1,0:T(8,128)(2,1)} %get-tuple-element.11.refs_1_, ...), custom_call_target="tpu_custom_call" | custom-call | tf_op jit(solution)/shard_map/pallas_call | solution.py:527
